TPU v7x, 768 devices: a whole 4x8x12 slice. The times are simulated.
768 devices in a mesh: dpx: 8 (over y_hi, x), dpy: 96 (over y_lo, z, core).
Axes of the slice: x: 4, y: 8 (y_hi: 2, y_lo: 4; y = y_hi * 4 + y_lo), z: 12, core: 2. Of those that a mesh axis runs over, the one named last changes fastest.
Arguments:
- tokens: bfloat16 [294912, 4608], P(('dpx', 'dpy')), may hold values from -24 to 24
- cotangents: bfloat16 [2, 294912, 128], P(None, ('dpx', 'dpy')), may hold values from -0.02734375 to 0.02734375
- params: float32 [2, 4608, 128], P(None, ('dpx', 'dpy')), may hold values from -0.75 to 0.75
- moment: float32 [2, 4608, 128], P(None, ('dpx', 'dpy')), may hold values from -4 to 4
- second: float32 [2, 4608, 128], P(None, ('dpx', 'dpy')), may hold values from 0.01 to 1
Outputs:
- new_params: float32 [2, 4608, 128], P(None, ('dpx', 'dpy'))
- new_moment: float32 [2, 4608, 128], P(None, ('dpx', 'dpy'))
- new_second: float32 [2, 4608, 128], P(None, ('dpx', 'dpy'))
- gathered: bfloat16 [2, 4608, 128], replicated
All inputs are finite; a program needn't handle non-finite values.
Results may differ from a plain program's by a relative error of at most 0.0059.
Values may be sent and summed in bfloat16 or wider, within the bound.
No kernel may reach another device: no remote copies, remote signals or barrier semaphores. Data moves between devices by JAX's collectives and lax.ppermute only.
A program may use at most 32 MiB of HBM per device.

v0:
```python
import jax
import jax.numpy as jnp
from jax import lax
from jax.sharding import PartitionSpec as P


def reduce_rows(gradient):
    partial_sum = lax.psum_scatter(
        gradient.astype(jnp.bfloat16), "dpx", scatter_dimension=0, tiled=True
    ).astype(jnp.float32)
    return lax.psum_scatter(partial_sum, "dpy", scatter_dimension=0, tiled=True)


def local_gradient(tokens, cotangent):
    return lax.dot_general(
        tokens, cotangent, (((0,), (0,)), ((), ())), preferred_element_type=jnp.float32
    )


def on_device(tokens, cotangents, params, moment, second):
    count = cotangents.shape[0]
    gradient = jnp.stack(
        [reduce_rows(local_gradient(tokens, cotangents[index])) for index in range(count)]
    )
    new_moment = 0.9 * moment + 0.1 * gradient
    new_second = 0.95 * second + 0.05 * gradient * gradient
    first_fix = 1.0 - 0.9**10
    second_fix = 1.0 - 0.95**10
    update = new_moment / first_fix / (jnp.sqrt(new_second / second_fix) + 1e-08)
    new_params = params - 0.01 * (update + 0.1 * params)
    rounded = new_params.astype(jnp.bfloat16)
    block_rows = lax.all_gather(rounded, "dpy", axis=1, tiled=True)
    gathered = lax.all_gather(block_rows, "dpx", axis=1, tiled=True)
    return (new_params, new_moment, new_second, gathered)


def solution(mesh):
    in_specs = (
        P(("dpx", "dpy"), None),
        P(None, ("dpx", "dpy"), None),
        P(None, ("dpx", "dpy"), None),
        P(None, ("dpx", "dpy"), None),
        P(None, ("dpx", "dpy"), None),
    )
    out_specs = (
        P(None, ("dpx", "dpy"), None),
        P(None, ("dpx", "dpy"), None),
        P(None, ("dpx", "dpy"), None),
        P(),
    )
    return jax.shard_map(
        on_device, mesh=mesh, in_specs=in_specs, out_specs=out_specs, check_vma=False
    )
```

profile of v0, /device:TPU:1, one launch (start us, length us, event | category | flops | bytes accessed | tf_op | source)
XLA Modules:
  0.0 833.1 jit_solution(9788769707732752755)
XLA Ops:
  7.2 0.0 copy-start
  7.2 0.0 reduce-scatter.5.cloned.1.call-start
  7.2 1.9 copy-done
  9.2 3.0 convolution_convert_fusion
  12.2 0.0 reduce-scatter.5.cloned.1.call-update
  12.2 0.0 reduce-scatter.3.cloned.1.call-start
  12.3 3.0 convolution_convert_fusion.1
  15.3 0.0 reduce-scatter.3.cloned.1.call-update
  15.3 0.0 all-gather.2.cloned.1.call-start
  15.4 1.3 dynamic-slice
  17.3 100.4 %reduce-scatter.5.cloned.1.call-done = bf16[576,128]{1,0:T(8,128)(2,1)} async-done(((bf16[4608,128]{1,0:T(8,128)(2,1)}), bf16[576,128]{1,0:T(8,128)(2,1)}) %reduce-scatter.5.cloned.1.call-update) | async-done | bytes 147472 | tf_op jit(solution)/shard_map/reduce_scatter | solution.py:8
  117.7 100.4 %reduce-scatter.3.cloned.1.call-done = bf16[576,128]{1,0:T(8,128)(2,1)} async-done(((bf16[4608,128]{1,0:T(8,128)(2,1)}), bf16[576,128]{1,0:T(8,128)(2,1)}) %reduce-scatter.3.cloned.1.call-update) | async-done | bytes 147472 | tf_op jit(solution)/shard_map/reduce_scatter | solution.py:8
  218.1 401.5 %all-reduce.4 = (f32[576,128]{1,0:T(8,128)}, f32[576,128]{1,0:T(8,128)}) all-reduce(bf16[576,128]{1,0:T(8,128)(2,1)} %reduce-scatter.5.cloned.1.call-done, bf16[576,128]{1,0:T(8,128)(2,1)} %reduce-scatter.3.cloned.1.call-done), channel_id=5, replica_groups=mesh['dpx'=8,'dpy'=96] {'dpy'}, use_global_device_ids=true, to_apply=%region_3.0.clone | all-reduce | flops 147456 | bytes 884736
  619.7 0.7 dynamic-slice_bitcast_fusion
  620.4 1.4 fusion.8
  621.7 124.3 %all_gather.6 = bf16[2,576,128]{2,0,1:T(2,128)(2,1)} all-gather(bf16[2,6,128]{2,0,1:T(2,128)(2,1)S(1)} %copy.29), channel_id=1, replica_groups=mesh['dpx'=8,'dpy'=96] {'dpy'}, dimensions={1}, use_global_device_ids=true | all-gather | bytes 297984 | tf_op jit(solution)/shard_map/all_gather | solution.py:32
  746.0 0.0 all-gather.2.cloned.1.call-update
  746.0 1.3 copy.30
  747.3 0.6 copy.31
  747.9 0.6 copy.32
  748.5 74.7 %all-gather.2.cloned.1.call-done = bf16[2,4608,128]{2,0,1:T(2,128)(2,1)} async-done(((bf16[2,576,128]{2,0,1:T(2,128)(2,1)}), bf16[2,4608,128]{2,0,1:T(2,128)(2,1)}) %all-gather.2.cloned.1.call-update) | async-done | bytes 2359312 | tf_op jit(solution)/shard_map/all_gather | solution.py:33
  823.2 3.4 copy.33
  (1 shorter events, 0.0 us)
Async XLA Ops:
  7.2 2.0 copy-start
  7.2 110.5 %reduce-scatter.5.cloned.1.call-start = ((), (), s32[]{:S(2)}) async-start(), calls=%async_computation.3 | async-start | bytes 1327104 | tf_op jit(solution)/shard_map/reduce_scatter | solution.py:8
  12.2 205.9 %reduce-scatter.3.cloned.1.call-start = ((), (), s32[]{:S(2)}) async-start(), calls=%async_computation.2 | async-start | bytes 1327104 | tf_op jit(solution)/shard_map/reduce_scatter | solution.py:8
  15.3 807.8 %all-gather.2.cloned.1.call-start = ((), (), s32[]{:S(2)}) async-start(), calls=%async_computation.4 | async-start | bytes 2654208 | tf_op jit(solution)/shard_map/all_gather | solution.py:33
Sparse Core Ops, SparseCore 0:
  13.8 103.8 reduce-scatter.4
  123.7 94.3 reduce-scatter.2
  746.1 76.9 all-gather.1
where the time goes:
time: 835 us; the launch traced here: 833 us
  blocking collectives  526 us (63%)
  waiting for transfers between devices  276 us (33%)
  between operations  14.4 us (2%)
  local copies, waits for them, and re-layouts  9.81 us (1%)
    unnamed x1, blocking collectives  402 us
    reduce_scatter x2, waiting for transfers between devices, reduce_rows(): lax.psum_scatter(gradient.astype(jnp.bfloat16), 'dpx', scatter_dimension=...  201 us
    all_gather x1, blocking collectives, on_device(): block_rows = lax.all_gather(rounded, 'dpy', axis=1, tiled=True)  124 us
    all_gather x1, waiting for transfers between devices, on_device(): gathered = lax.all_gather(block_rows, 'dpx', axis=1, tiled=True)  74.7 us
  transfers between devices with their start and end apart: 3, of which 3 were waited for; matrix products, arithmetic and copies ran while one was open for 1% of the time, Pallas kernels for 0%

commit v1 on v0

v1 whole, which is shorter than its diff:
```python
import jax
import jax.numpy as jnp
from jax import lax
from jax.sharding import Mesh
from jax.sharding import PartitionSpec as P

ALL = ("yh", "x", "yl", "yp", "z", "core")
SIZES = (2, 4, 2, 2, 12, 2)
NEAR = ("x", "yp")
FAR = ("yh", "yl", "z")
SWAP = [(0, 1), (1, 0)]


def exchange(blocks, axes):
    return lax.all_to_all(blocks, axes, 0, 0, tiled=True)


def total(blocks):
    return blocks.astype(jnp.float32).sum(0)


def adam(gradient, params, moment, second):
    new_moment = 0.9 * moment + 0.1 * gradient
    new_second = 0.95 * second + 0.05 * gradient * gradient
    first_fix = 1.0 - 0.9**10
    second_fix = 1.0 - 0.95**10
    update = new_moment / first_fix / (jnp.sqrt(new_second / second_fix) + 1e-08)
    new_params = params - 0.01 * (update + 0.1 * params)
    return new_params, new_moment, new_second


def on_device(tokens, cotangents, params, moment, second):
    core = lax.axis_index("core")

    def local_gradient(bucket):
        cotangent = lax.dynamic_index_in_dim(cotangents, bucket, 0, False)
        return lax.dot_general(
            tokens, cotangent, (((0,), (0,)), ((), ())), preferred_element_type=jnp.float32
        ).astype(jnp.bfloat16)

    away = lax.ppermute(local_gradient(1 - core), "core", SWAP)
    state = jnp.stack([params, moment, second])
    away_state = lax.dynamic_index_in_dim(state, 1 - core, 1, False)
    home_state = lax.dynamic_index_in_dim(state, core, 1, False)
    other_state = lax.ppermute(away_state, "core", SWAP)
    home = lax.optimization_barrier(local_gradient(core))
    part = (home.astype(jnp.float32) + away.astype(jnp.float32)).astype(jnp.bfloat16)

    near = part.reshape(2, 4, 2, 2, 144, 128).transpose(1, 3, 0, 2, 4, 5).reshape(8, 576, 128)
    near = total(exchange(near, NEAR)).astype(jnp.bfloat16)
    gradient = total(exchange(near.reshape(48, 12, 128), FAR))

    first = core == 0
    rows_state = jnp.where(
        first,
        jnp.concatenate([home_state, other_state], axis=1),
        jnp.concatenate([other_state, home_state], axis=1),
    )
    rounded = adam(gradient, *rows_state)[0].astype(jnp.bfloat16)

    keep = jnp.where(first, gradient[:6], gradient[6:])
    other = lax.ppermute(jnp.where(first, gradient[6:], gradient[:6]), "core", SWAP)
    both = jnp.where(first, jnp.stack([keep, other]), jnp.stack([other, keep]))
    new_params, new_moment, new_second = adam(both, params, moment, second)

    far = exchange(jnp.broadcast_to(rounded, (48, 12, 128)), FAR).reshape(576, 128)
    near = exchange(jnp.broadcast_to(far, (8, 576, 128)), NEAR)
    mine = near.reshape(4, 2, 2, 2, 144, 128).transpose(2, 0, 3, 1, 4, 5).reshape(4608, 128)
    theirs = lax.ppermute(mine, "core", SWAP)
    gathered = jnp.where(first, jnp.stack([mine, theirs]), jnp.stack([theirs, mine]))
    return (new_params, new_moment, new_second, gathered)


def solution(mesh):
    fine = Mesh(mesh.devices.reshape(SIZES), ALL)
    rows = P(None, ALL, None)
    return jax.shard_map(
        on_device,
        mesh=fine,
        in_specs=(P(ALL, None), rows, rows, rows, rows),
        out_specs=(rows, rows, rows, P()),
        check_vma=False,
    )
```

time: 835 us -> 136 us (0.16)
  blocking collectives: 526 us -> 58.3 us
  waiting for transfers between devices: 276 us -> 10.6 us
  starting transfers between devices: 0.12 us -> 37.5 us
  between operations: 14.4 us -> 0.83 us
  other arithmetic: 1.35 us -> 10.3 us
    unnamed x1 -> x0, blocking collectives: 402 us -> none
    reduce_scatter x2 -> x0, waiting for transfers between devices: 201 us -> none  [reduce_rows(): lax.psum_scatter(gradient.astype(jnp.bfloat16), 'dpx', scatter_dimension=...]
    all_gather x1 -> x0, blocking collectives: 124 us -> none  [on_device(): block_rows = lax.all_gather(rounded, 'dpy', axis=1, tiled=True)]
    all_gather x1 -> x0, waiting for transfers between devices: 74.7 us -> none  [on_device(): gathered = lax.all_gather(block_rows, 'dpx', axis=1, tiled=True)]
    all_to_all x0 -> x3, blocking collectives: none -> 58.3 us  [exchange(): return lax.all_to_all(blocks, axes, 0, 0, tiled=True)]
    ppermute x0 -> x4, starting transfers between devices: none -> 25.2 us  [the longest x1 12.4 us: on_device(): away = lax.ppermute(local_gradient(1 - core), 'core', SWAP)]
    all_to_all x0 -> x1, starting transfers between devices: none -> 12.3 us  [exchange(): return lax.all_to_all(blocks, axes, 0, 0, tiled=True)]
  transfers between devices with their start and end apart: 3 -> 5, of which waited for: 3 -> 4; matrix products, arithmetic and copies ran while one was open for 1% -> 5% of each run, Pallas kernels for 0% -> 0%
where the time goes in v1:
time: 136 us; the launch traced here: 135 us
  blocking collectives  58.3 us (43%)
  starting transfers between devices  37.5 us (28%)
  local copies, waits for them, and re-layouts  12.6 us (9%)
  waiting for transfers between devices  10.6 us (8%)
  other arithmetic  10.3 us (8%)
  matrix products  4.41 us (3%)
    all_to_all x3, blocking collectives, exchange(): return lax.all_to_all(blocks, axes, 0, 0, tiled=True)  58.3 us
    ppermute x1, starting transfers between devices, on_device(): away = lax.ppermute(local_gradient(1 - core), 'core', SWAP)  12.4 us
    all_to_all x1, starting transfers between devices, exchange(): return lax.all_to_all(blocks, axes, 0, 0, tiled=True)  12.3 us
    all_to_all x1, waiting for transfers between devices, exchange(): return lax.all_to_all(blocks, axes, 0, 0, tiled=True)  7.27 us
    ppermute x1, starting transfers between devices, on_device(): theirs = lax.ppermute(mine, 'core', SWAP)  6.74 us
    unnamed x17, local copies, waits for them, and re-layouts  4.42 us
    dot_general x2, matrix products, local_gradient(): lax.dot_general(tokens, cotangent, (((0,), (0,)), ((), ())), preferred_el...  4.41 us
    ppermute x1, starting transfers between devices, on_device(): other_state = lax.ppermute(away_state, 'core', SWAP)  4.08 us
  transfers between devices with their start and end apart: 5, of which 4 were waited for; matrix products, arithmetic and copies ran while one was open for 5% of the time, Pallas kernels for 0%

profile of v1, /device:TPU:1, one launch (start us, length us, event | category | flops | bytes accessed | tf_op | source)
XLA Modules:
  0.0 134.6 jit_solution(3420461155712074626)
XLA Ops:
  0.6 0.0 copy-start
  0.6 2.0 %copy-done = bf16[384,4608]{1,0:T(8,128)(2,1)S(1)} copy-done((bf16[384,4608]{1,0:T(8,128)(2,1)S(1)}, bf16[384,4608]{1,0:T(8,128)(2,1)}, u32[]{:S(2)}) %copy-start) | copy-done | bytes 3538968
  2.6 2.7 %fusion.1 = bf16[4608,128]{0,1:T(8,128)(2,1)} fusion(bf16[384,4608]{1,0:T(8,128)(2,1)S(1)} %copy-done, bf16[2,384,128]{2,1,0:T(8,128)(2,1)} %param.6, s32[]{:T(128)S(6)} %select_n.49), kind=kOutput, calls=%fused_computation.3 | convolution fusion | flops 453574656 | bytes 4816900 | tf_op jit(solution)/shard_map/dot_general | solution.py:37
  5.3 12.4 %collective-permute-start = (bf16[4608,128]{0,1:T(8,128)(2,1)}, bf16[4608,128]{0,1:T(8,128)(2,1)}, u32[]{:S(2)}, u32[]{:S(2)}) collective-permute-start(bf16[4608,128]{0,1:T(8,128)(2,1)} %fusion.1), channel_id=1, source_target_pairs={{0,1},{1,0},{2,3},{3,2},{4,5},{5,4},{6,7},{7,6},{8,9},{9,8},{10,11... | collective-permute-start | bytes 3538952 | tf_op jit(solution)/shard_map/ppermute | solution.py:41
  17.8 1.7 %fusion = bf16[4608,128]{0,1:T(8,128)(2,1)S(1)} fusion(bf16[384,4608]{1,0:T(8,128)(2,1)S(1)} %copy-done, bf16[2,384,128]{2,1,0:T(8,128)(2,1)} %param.6, s32[]{:T(128)S(6)} %select_n.48), kind=kOutput, calls=%fused_computation.2 | convolution fusion | flops 453574656 | bytes 4816900 | tf_op jit(solution)/shard_map/dot_general | solution.py:37
  19.5 1.1 collective-permute-done
  20.6 2.6 %add_convert_fusion = bf16[4608,128]{0,1:T(8,128)(2,1)} fusion(bf16[4608,128]{0,1:T(8,128)(2,1)} %collective-permute-done, bf16[4608,128]{0,1:T(8,128)(2,1)S(1)} %fusion), kind=kLoop, calls=%fused_computation.5 | loop fusion | flops 2359296 | bytes 3538944 | tf_op jit(solution)/shard_map/convert_element_type | solution.py:47
  23.1 2.4 %copy.19 = bf16[4608,128]{1,0:T(8,128)(2,1)} copy(bf16[4608,128]{0,1:T(8,128)(2,1)} %add_convert_fusion) | data formatting | bytes 2359296 | tf_op jit(solution)/shard_map/convert_element_type | solution.py:47
  25.5 1.4 %copy.20 = bf16[4,2,2,2,144,128]{5,4,3,2,1,0:T(8,128)(2,1)S(1)} copy(bf16[4,2,2,2,144,128]{5,4,1,3,0,2:T(8,128)(2,1)} %bitcast.58) | data formatting | bytes 2359296 | tf_op jit(solution)/shard_map/transpose | solution.py:49
  26.9 0.0 copy-start.1
  26.9 0.0 copy-start.3
  26.9 20.0 %all_to_all.20 = bf16[8,576,128]{2,1,0:T(8,128)(2,1)} all-to-all(bf16[8,576,128]{2,1,0:T(8,128)(2,1)S(1)} %bitcast.59), channel_id=1, replica_groups=mesh['yh'=2,'x'=4,'yl'=2,'yp'=2,'z'=12,'core'=2] {'x','yp'}, dimensions={0} | all-to-all | bytes 2359296 | tf_op jit(solution)/shard_map/all_to_all | solution.py:15
  46.9 2.1 %reduce_sum.21 = bf16[576,128]{1,0:T(8,128)(2,1)} reduce(bf16[8,576,128]{2,1,0:T(8,128)(2,1)} %all_to_all.20, bf16[]{:T(256)} %constant.21.clone.1), dimensions={0}, to_apply=%region_0.1 | reduce | flops 516096 | bytes 1327106 | tf_op jit(solution)/shard_map/reduce_sum | solution.py:19
  49.0 1.6 %reshape.32 = bf16[48,12,128]{2,1,0:T(8,128)(2,1)} reshape(bf16[576,128]{1,0:T(8,128)(2,1)} %reduce_sum.21) | data formatting | bytes 294912 | tf_op jit(solution)/shard_map/reshape | solution.py:51
  50.6 12.3 %all-to-all-start.1 = ((bf16[48,12,128]{2,1,0:T(8,128)(2,1)}), bf16[48,12,128]{2,1,0:T(8,128)(2,1)}, u32[]{:S(2)}, u32[]{:S(2)}) async-start(bf16[48,12,128]{2,1,0:T(8,128)(2,1)} %reshape.32), calls=%async_computation.1 | async-start | bytes 393216 | tf_op jit(solution)/shard_map/all_to_all | solution.py:15
  63.0 0.0 copy-done.1
  63.0 0.0 copy-done.3
  63.0 0.7 pad_maximum_fusion
  63.7 0.6 copy.49
  64.3 4.1 %collective-permute-start.2 = (f32[3,6,128]{2,1,0:T(8,128)}, f32[3,6,128]{2,1,0:T(8,128)}, u32[]{:S(2)}, u32[]{:S(2)}) collective-permute-start(f32[3,6,128]{2,1,0:T(8,128)} %bitcast.54), channel_id=1, source_target_pairs={{0,1},{1,0},{2,3},{3,2},{4,5},{5,4},{6,7},{7,6},{8,9},{9,8},{10,11... | collective-permute-start | bytes 27656 | tf_op jit(solution)/shard_map/ppermute | solution.py:45
  68.4 1.1 collective-permute-done.2
  69.6 1.4 %maximum_select_fusion.1 = f32[3,12,128]{2,1,0:T(8,128)} fusion(f32[3,6,128]{2,1,0:T(8,128)} %collective-permute-done.2, f32[3,6,128]{2,1,0:T(8,128)S(1)} %bitcast.62, pred[]{:T(512)S(6)} %eq.3), kind=kLoop, calls=%fused_computation.11 | loop fusion | flops 13824 | bytes 36865 | tf_op jit(solution)/shard_map/jit(_where)/select_n | solution.py:54
  71.0 7.3 %all-to-all-done.1 = bf16[48,12,128]{2,1,0:T(8,128)(2,1)} async-done(((bf16[48,12,128]{2,1,0:T(8,128)(2,1)}), bf16[48,12,128]{2,1,0:T(8,128)(2,1)}, u32[]{:S(2)}, u32[]{:S(2)}) %all-to-all-start.1) | async-done | bytes 147488 | tf_op jit(solution)/shard_map/all_to_all | solution.py:15
  78.2 1.0 convert_reduce_fusion
  79.2 0.8 fusion.22
  80.0 22.5 %all_to_all.21 = bf16[48,12,128]{2,1,0:T(8,128)(2,1)} all-to-all(bf16[48,12,128]{2,1,0:T(8,128)(2,1)S(1)} %broadcast_in_dim.6), channel_id=1, replica_groups=mesh['yh'=2,'x'=4,'yl'=2,'yp'=2,'z'=12,'core'=2] {'yh','yl','z'}, dimensions={0} | all-to-all | bytes 294912 | tf_op jit(solution)/shard_map/all_to_all | solution.py:15
  102.5 1.6 %reshape.33 = bf16[576,128]{1,0:T(8,128)(2,1)} reshape(bf16[48,12,128]{2,1,0:T(8,128)(2,1)} %all_to_all.21) | data formatting | bytes 294912 | tf_op jit(solution)/shard_map/reshape | solution.py:66
  104.1 1.1 broadcast_in_dim.7
  105.2 0.0 copy-start.2
  105.2 0.0 copy-start.4
  105.2 0.0 copy-start.5
  105.2 15.9 %all_to_all.22 = bf16[8,576,128]{2,1,0:T(8,128)(2,1)S(1)} all-to-all(bf16[8,576,128]{2,1,0:T(8,128)(2,1)S(1)} %broadcast_in_dim.7), channel_id=1, replica_groups=mesh['yh'=2,'x'=4,'yl'=2,'yp'=2,'z'=12,'core'=2] {'x','yp'}, dimensions={0} | all-to-all | bytes 2359296 | tf_op jit(solution)/shard_map/all_to_all | solution.py:15
  121.1 0.1 copy.24
  121.2 6.7 %collective-permute-start.3 = (bf16[4608,128]{1,0:T(8,128)(2,1)S(1)}, bf16[4608,128]{1,0:T(8,128)(2,1)S(1)}, u32[]{:S(2)}, u32[]{:S(2)}) collective-permute-start(bf16[4608,128]{1,0:T(8,128)(2,1)S(1)} %bitcast.56), channel_id=1, source_target_pairs={{0,1},{1,0},{2,3},{3,2},{4,5},{5,4},{6,7},{7,6},{8,9},{9,8},{10,11... | collective-permute-start | bytes 3538952 | tf_op jit(solution)/shard_map/ppermute | solution.py:69
  128.0 1.9 %collective-permute-start.1 = (f32[6,128]{1,0:T(8,128)S(1)}, f32[6,128]{1,0:T(8,128)S(1)}, u32[]{:S(2)}, u32[]{:S(2)}) collective-permute-start(f32[6,128]{1,0:T(8,128)S(1)} %get-tuple-element.17), channel_id=1, source_target_pairs={{0,1},{1,0},{2,3},{3,2},{4,5},{5,4},{6,7},{7,6},{8,9},{9,8},{10,11... | collective-permute-start | bytes 9224 | tf_op jit(solution)/shard_map/ppermute | solution.py:62
  129.9 1.1 collective-permute-done.1
  131.0 0.0 copy-done.2
  131.0 0.0 copy-done.4
  131.0 0.0 copy-done.5
  131.1 0.6 copy.26
  131.7 0.6 copy.27
  132.3 0.6 copy.28
  132.9 0.0 collective-permute-done.3
  132.9 1.8 %maximum_select_fusion = bf16[2,4608,128]{2,1,0:T(8,128)(2,1)} fusion(bf16[1,4608,128]{2,1,0:T(8,128)(2,1)S(1)} %bitcast.61, bf16[1,4608,128]{2,1,0:T(8,128)(2,1)S(1)} %bitcast.57, pred[]{:T(512)S(6)} %eq.3), kind=kLoop, calls=%fused_computation.4 | loop fusion | flops 3538944 | bytes 4718593 | tf_op jit(solution)/shard_map/jit(_where)/select_n | solution.py:70
  (5 shorter events, 0.1 us)
Async XLA Ops:
  0.6 2.0 %copy-start = (bf16[384,4608]{1,0:T(8,128)(2,1)S(1)}, bf16[384,4608]{1,0:T(8,128)(2,1)}, u32[]{:S(2)}) copy-start(bf16[384,4608]{1,0:T(8,128)(2,1)} %param.5) | copy-start | bytes 10616836
  5.3 15.2 %collective-permute-start = (bf16[4608,128]{0,1:T(8,128)(2,1)}, bf16[4608,128]{0,1:T(8,128)(2,1)}, u32[]{:S(2)}, u32[]{:S(2)}) collective-permute-start(bf16[4608,128]{0,1:T(8,128)(2,1)} %fusion.1), channel_id=1, source_target_pairs={{0,1},{1,0},{2,3},{3,2},{4,5},{5,4},{6,7},{7,6},{8,9},{9,8},{10,11... | collective-permute-start | bytes 3538952 | tf_op jit(solution)/shard_map/ppermute | solution.py:41
  26.9 36.1 %copy-start.1 = (f32[2,6,128]{2,0,1:T(2,128)S(1)}, f32[2,6,128]{2,0,1:T(2,128)}, u32[]{:S(2)}) copy-start(f32[2,6,128]{2,0,1:T(2,128)} %param.7) | copy-start | bytes 18436
  26.9 36.1 %copy-start.3 = (f32[2,6,128]{2,0,1:T(2,128)S(1)}, f32[2,6,128]{2,0,1:T(2,128)}, u32[]{:S(2)}) copy-start(f32[2,6,128]{2,0,1:T(2,128)} %param.8) | copy-start | bytes 18436
  50.6 27.6 %all-to-all-start.1 = ((bf16[48,12,128]{2,1,0:T(8,128)(2,1)}), bf16[48,12,128]{2,1,0:T(8,128)(2,1)}, u32[]{:S(2)}, u32[]{:S(2)}) async-start(bf16[48,12,128]{2,1,0:T(8,128)(2,1)} %reshape.32), calls=%async_computation.1 | async-start | bytes 393216 | tf_op jit(solution)/shard_map/all_to_all | solution.py:15
  64.3 5.2 %collective-permute-start.2 = (f32[3,6,128]{2,1,0:T(8,128)}, f32[3,6,128]{2,1,0:T(8,128)}, u32[]{:S(2)}, u32[]{:S(2)}) collective-permute-start(f32[3,6,128]{2,1,0:T(8,128)} %bitcast.54), channel_id=1, source_target_pairs={{0,1},{1,0},{2,3},{3,2},{4,5},{5,4},{6,7},{7,6},{8,9},{9,8},{10,11... | collective-permute-start | bytes 27656 | tf_op jit(solution)/shard_map/ppermute | solution.py:45
  105.2 25.8 %copy-start.2 = (f32[2,6,128]{2,0,1:T(2,128)S(1)}, f32[2,6,128]{2,0,1:T(2,128)}, u32[]{:S(2)}) copy-start(f32[2,6,128]{2,0,1:T(2,128)} %param.7) | copy-start | bytes 18436
  105.2 25.8 %copy-start.4 = (f32[2,6,128]{2,0,1:T(2,128)S(1)}, f32[2,6,128]{2,0,1:T(2,128)}, u32[]{:S(2)}) copy-start(f32[2,6,128]{2,0,1:T(2,128)} %param.8) | copy-start | bytes 18436
  105.2 25.8 %copy-start.5 = (f32[2,6,128]{2,0,1:T(2,128)S(1)}, f32[2,6,128]{2,0,1:T(2,128)}, u32[]{:S(2)}) copy-start(f32[2,6,128]{2,0,1:T(2,128)} %param.9) | copy-start | bytes 18436
  121.2 11.7 %collective-permute-start.3 = (bf16[4608,128]{1,0:T(8,128)(2,1)S(1)}, bf16[4608,128]{1,0:T(8,128)(2,1)S(1)}, u32[]{:S(2)}, u32[]{:S(2)}) collective-permute-start(bf16[4608,128]{1,0:T(8,128)(2,1)S(1)} %bitcast.56), channel_id=1, source_target_pairs={{0,1},{1,0},{2,3},{3,2},{4,5},{5,4},{6,7},{7,6},{8,9},{9,8},{10,11... | collective-permute-start | bytes 3538952 | tf_op jit(solution)/shard_map/ppermute | solution.py:69
  128.0 3.1 %collective-permute-start.1 = (f32[6,128]{1,0:T(8,128)S(1)}, f32[6,128]{1,0:T(8,128)S(1)}, u32[]{:S(2)}, u32[]{:S(2)}) collective-permute-start(f32[6,128]{1,0:T(8,128)S(1)} %get-tuple-element.17), channel_id=1, source_target_pairs={{0,1},{1,0},{2,3},{3,2},{4,5},{5,4},{6,7},{7,6},{8,9},{9,8},{10,11... | collective-permute-start | bytes 9224 | tf_op jit(solution)/shard_map/ppermute | solution.py:62

commit v2 on v1

v2 whole, which is shorter than its diff:
```python
import functools

import jax
import jax.numpy as jnp
import numpy as np
from jax import lax
from jax.experimental import pallas as pl
from jax.experimental.pallas import tpu as pltpu
from jax.sharding import Mesh
from jax.sharding import PartitionSpec as P

ALL = ("yh", "x", "yl", "yp", "zl", "zp", "core")
SIZES = (2, 4, 2, 2, 6, 2, 2)
NEAR = ("x", "yp", "zp")
FAR = ("yh", "yl", "zl")
N_NEAR, N_FAR = 16, 24
SWAP = [(0, 1), (1, 0)]
ROWS = 6
HALF = 2304
CHUNK = 768
COLS = 128

_at = np.indices(SIZES).reshape(len(SIZES), -1)
_at = dict(zip(ALL, _at))
HOLDS = (
    _at["core"] * (N_NEAR * N_FAR)
    + ((_at["x"] * 2 + _at["yp"]) * 2 + _at["zp"]) * N_FAR
    + (_at["yh"] * 2 + _at["yl"]) * 6
    + _at["zl"]
)
TO_OWNER = [(holder, int(owner)) for holder, owner in enumerate(HOLDS)]
TO_HOLDER = [(owner, holder) for holder, owner in TO_OWNER]

VMEM = pl.BlockSpec(memory_space=pltpu.VMEM)


def exchange(blocks, axes):
    return lax.all_to_all(blocks, axes, 0, 0, tiled=True)


def total(blocks):
    return blocks.astype(jnp.float32).sum(0)


def gradient_kernel(other, tokens, cotangents, out, held, arrived):
    core = lax.axis_index("core")
    half = 1 - core if other else core
    copies = []
    for step in range(HALF // CHUNK):
        first = pl.multiple_of(half * HALF + step * CHUNK, COLS)
        copies.append(
            pltpu.make_async_copy(
                tokens.at[:, pl.ds(first, CHUNK)], held.at[step], arrived.at[step]
            )
        )
        copies[-1].start()
    both = jnp.concatenate([cotangents[0], cotangents[1]], axis=1)
    for step, copy in enumerate(copies):
        copy.wait()
        out[step * CHUNK : (step + 1) * CHUNK, :] = lax.dot_general(
            held[step], both, (((0,), (0,)), ((), ())), preferred_element_type=jnp.float32
        ).astype(out.dtype)


def local_gradient(tokens, cotangents, other):
    count = tokens.shape[0]
    return pl.pallas_call(
        functools.partial(gradient_kernel, other),
        out_shape=jax.ShapeDtypeStruct((HALF, 2 * COLS), jnp.bfloat16),
        in_specs=[pl.BlockSpec(memory_space=pltpu.HBM), VMEM],
        out_specs=VMEM,
        scratch_shapes=[
            pltpu.VMEM((HALF // CHUNK, count, CHUNK), jnp.bfloat16),
            pltpu.SemaphoreType.DMA((HALF // CHUNK,)),
        ],
        compiler_params=pltpu.CompilerParams(vmem_limit_bytes=60_000_000),
        cost_estimate=pl.CostEstimate(
            flops=2 * count * HALF * 2 * COLS, bytes_accessed=count * HALF * 2, transcendentals=0
        ),
        name="gradient_kernel",
    )(tokens, cotangents)


def sum_kernel(blocks, out, held):
    held[...] = blocks[...].astype(jnp.float32).sum(0)
    for index in range(N_FAR):
        out[index] = held[index * ROWS : (index + 1) * ROWS, :].astype(out.dtype)


def sum_near(blocks):
    return pl.pallas_call(
        sum_kernel,
        out_shape=jax.ShapeDtypeStruct((N_FAR, ROWS, 2 * COLS), jnp.bfloat16),
        in_specs=[VMEM],
        out_specs=VMEM,
        scratch_shapes=[pltpu.VMEM((N_FAR * ROWS, 2 * COLS), jnp.float32)],
        compiler_params=pltpu.CompilerParams(vmem_limit_bytes=24 * 2**20),
        name="sum_kernel",
    )(blocks)


def spread_kernel(blocks, out, held):
    for index in range(N_FAR):
        held[index * ROWS : (index + 1) * ROWS, :] = blocks[index].astype(jnp.float32)
    rows = held[...].astype(out.dtype)
    for index in range(N_NEAR):
        out[index] = rows


def spread_far(blocks):
    return pl.pallas_call(
        spread_kernel,
        out_shape=jax.ShapeDtypeStruct((N_NEAR, N_FAR * ROWS, 2 * COLS), jnp.bfloat16),
        in_specs=[VMEM],
        out_specs=VMEM,
        scratch_shapes=[pltpu.VMEM((N_FAR * ROWS, 2 * COLS), jnp.float32)],
        compiler_params=pltpu.CompilerParams(vmem_limit_bytes=24 * 2**20),
        name="spread_kernel",
    )(blocks)


def adam(gradient, params, moment, second):
    new_moment = 0.9 * moment + 0.1 * gradient
    new_second = 0.95 * second + 0.05 * gradient * gradient
    first_fix = 1.0 - 0.9**10
    second_fix = 1.0 - 0.95**10
    update = new_moment / first_fix / (jnp.sqrt(new_second / second_fix) + 1e-08)
    new_params = params - 0.01 * (update + 0.1 * params)
    return new_params, new_moment, new_second


def on_device(tokens, cotangents, params, moment, second):
    first = lax.axis_index("core") == 0

    away = lax.ppermute(local_gradient(tokens, cotangents, True), "core", SWAP)
    home = local_gradient(tokens, cotangents, False)
    part = (home.astype(jnp.float32) + away.astype(jnp.float32)).astype(jnp.bfloat16)

    state = jnp.stack([jnp.concatenate([a[0], a[1]], axis=1) for a in (params, moment, second)])
    state, part = lax.optimization_barrier((state, part))
    held = lax.ppermute(state, ALL, TO_HOLDER)

    near = exchange(part.reshape(N_NEAR, N_FAR * ROWS, 2 * COLS), NEAR)
    gradient = total(exchange(sum_near(near), FAR))
    rounded = adam(gradient, *held)[0].astype(jnp.bfloat16)

    far = exchange(jnp.broadcast_to(rounded, (N_FAR, ROWS, 2 * COLS)), FAR)

    owned = lax.ppermute(gradient, ALL, TO_OWNER)
    owned = jnp.stack([owned[:, :COLS], owned[:, COLS:]])
    new_params, new_moment, new_second = adam(owned, params, moment, second)

    mine = exchange(spread_far(far), NEAR).reshape(HALF, 2 * COLS)
    theirs = lax.ppermute(mine, "core", SWAP)
    rows = jnp.concatenate([jnp.where(first, mine, theirs), jnp.where(first, theirs, mine)])
    gathered = jnp.stack([rows[:, :COLS], rows[:, COLS:]])
    return (new_params, new_moment, new_second, gathered)


def solution(mesh):
    fine = Mesh(mesh.devices.reshape(SIZES), ALL)
    rows = P(None, ALL, None)
    return jax.shard_map(
        on_device,
        mesh=fine,
        in_specs=(P(ALL, None), rows, rows, rows, rows),
        out_specs=(rows, rows, rows, P()),
        check_vma=False,
    )
```

time: 136 us -> 133 us (0.978)
  the two profiles are of different devices: /device:TPU:1 before, /device:TPU:73 now
where the time goes in v2:
time: 133 us; the launch traced here: 132 us
  blocking collectives  65.7 us (49%)
  starting transfers between devices  37.6 us (28%)
  waiting for transfers between devices  12.2 us (9%)
  Pallas kernels  10.2 us (8%)
  other arithmetic  3.71 us (3%)
  local copies, waits for them, and re-layouts  1.83 us (1%)
    all_to_all x3, blocking collectives, exchange(): return lax.all_to_all(blocks, axes, 0, 0, tiled=True)  65.7 us
    all_to_all x1, starting transfers between devices, exchange(): return lax.all_to_all(blocks, axes, 0, 0, tiled=True)  12.4 us
    ppermute x1, starting transfers between devices, on_device(): held = lax.ppermute(state, ALL, TO_HOLDER)  11.7 us
    ppermute x1, waiting for transfers between devices, on_device(): owned = lax.ppermute(gradient, ALL, TO_OWNER)  9.44 us
    pallas_call x2, Pallas kernels, local_gradient(): pl.pallas_call(functools.partial(gradient_kernel, other), out_shape=jax.S...  9.25 us
    ppermute x1, starting transfers between devices, on_device(): theirs = lax.ppermute(mine, 'core', SWAP)  8.23 us
    all_to_all x1, waiting for transfers between devices, exchange(): return lax.all_to_all(blocks, axes, 0, 0, tiled=True)  2.79 us
    ppermute x1, starting transfers between devices, on_device(): owned = lax.ppermute(gradient, ALL, TO_OWNER)  2.72 us
  transfers between devices with their start and end apart: 5, of which 2 were waited for; matrix products, arithmetic and copies ran while one was open for 1% of the time, Pallas kernels for 4%

profile of v2, /device:TPU:73, one launch (start us, length us, event | category | flops | bytes accessed | tf_op | source)
XLA Modules:
  0.0 132.2 jit_solution(16221186474256302309)
XLA Ops:
  0.6 0.0 copy-start
  0.6 0.0 copy-start.1
  0.7 0.0 copy-start.2
  0.7 4.6 %gradient_kernel.3 = bf16[2304,256]{1,0:T(8,128)(2,1)} custom-call(bf16[384,4608]{1,0:T(8,128)(2,1)} %tokens.3, bf16[2,384,128]{2,1,0:T(8,128)(2,1)} %cotangents.3), custom_call_target="tpu_custom_call" | custom-call | flops 452984832 | bytes 1769472 | tf_op jit(solution)/shard_map/gradient_kernel/pallas_call | solution.py:67
  5.3 2.6 %collective-permute-start = (bf16[2304,256]{1,0:T(8,128)(2,1)}, bf16[2304,256]{1,0:T(8,128)(2,1)S(1)}, u32[]{:S(2)}, u32[]{:S(2)}) collective-permute-start(bf16[2304,256]{1,0:T(8,128)(2,1)} %gradient_kernel.3), channel_id=1, source_target_pairs={{0,1},{1,0},{2,3},{3,2},{4,5},{5,4},{6,7},{7,6},{8,9},{9,8},{10,11... | collective-permute-start | bytes 3538952 | tf_op jit(solution)/shard_map/ppermute | solution.py:135
  7.9 0.0 copy-done
  7.9 0.0 copy-done.1
  7.9 0.0 copy-done.2
  7.9 4.6 %gradient_kernel.2 = bf16[2304,256]{1,0:T(8,128)(2,1)} custom-call(bf16[384,4608]{1,0:T(8,128)(2,1)} %tokens.3, bf16[2,384,128]{2,1,0:T(8,128)(2,1)} %cotangents.3), custom_call_target="tpu_custom_call" | custom-call | flops 452984832 | bytes 1769472 | tf_op jit(solution)/shard_map/gradient_kernel/pallas_call | solution.py:67
  12.7 0.0 collective-permute-done
  12.7 1.6 %add_convert_fusion = bf16[2304,256]{1,0:T(8,128)(2,1)S(1)} fusion(bf16[2304,256]{1,0:T(8,128)(2,1)S(1)} %collective-permute-done, bf16[2304,256]{1,0:T(8,128)(2,1)} %gradient_kernel.2), kind=kLoop, calls=%fused_computation.3 | loop fusion | flops 2359296 | bytes 3538944 | tf_op jit(solution)/shard_map/convert_element_type | solution.py:137
  14.3 27.5 %all_to_all.20.blocks = bf16[16,144,256]{2,1,0:T(8,128)(2,1)S(1)} all-to-all(bf16[16,144,256]{2,1,0:T(8,128)(2,1)S(1)} %bitcast.53), channel_id=1, replica_groups=mesh['yh'=2,'x'=4,'yl'=2,'yp'=2,'zl'=6,'zp'=2,'core'=2] {'x','yp','zp'}, dimensions={0} | all-to-all | bytes 2359296 | tf_op jit(solution)/shard_map/all_to_all | solution.py:38
  41.8 0.9 sum_kernel.1
  42.6 12.4 %all-to-all-start.1 = ((bf16[24,6,256]{2,1,0:T(8,128)(2,1)}), bf16[24,6,256]{2,1,0:T(8,128)(2,1)S(1)}, u32[]{:S(2)}, u32[]{:S(2)}) async-start(bf16[24,6,256]{2,1,0:T(8,128)(2,1)} %sum_kernel.1), calls=%async_computation.1 | async-start | bytes 196608 | tf_op jit(solution)/shard_map/all_to_all | solution.py:38
  55.0 11.7 %collective-permute-start.2 = (f32[3,6,256]{2,1,0:T(8,128)S(1)}, f32[3,6,256]{2,1,0:T(8,128)S(1)}, u32[]{:S(2)}, u32[]{:S(2)}) collective-permute-start(f32[3,6,256]{2,1,0:T(8,128)S(1)} %pad_maximum_fusion.2), channel_id=1, source_target_pairs={{0,0},{384,1},{24,2},{408,3},{1,4},{385,5},{25,6},{409,7},{2,8},{3... | collective-permute-start | bytes 55304 | tf_op jit(solution)/shard_map/ppermute | solution.py:141
  66.8 2.8 %all-to-all-done.1 = bf16[24,6,256]{2,1,0:T(8,128)(2,1)S(1)} async-done(((bf16[24,6,256]{2,1,0:T(8,128)(2,1)}), bf16[24,6,256]{2,1,0:T(8,128)(2,1)S(1)}, u32[]{:S(2)}, u32[]{:S(2)}) %all-to-all-start.1) | async-done | bytes 73760 | tf_op jit(solution)/shard_map/all_to_all | solution.py:38
  69.6 0.0 collective-permute-done.2
  69.6 22.4 %all_to_all.21.blocks = bf16[24,6,256]{2,1,0:T(8,128)(2,1)S(1)} all-to-all(bf16[24,6,256]{2,1,0:T(8,128)(2,1)S(1)} %broadcast_in_dim.3), channel_id=1, replica_groups=mesh['yh'=2,'x'=4,'yl'=2,'yp'=2,'zl'=6,'zp'=2,'core'=2] {'yh','yl','zl'}, dimensions={0} | all-to-all | bytes 147456 | tf_op jit(solution)/shard_map/all_to_all | solution.py:38
  92.0 0.1 spread_kernel.1
  92.1 15.9 %all_to_all.22 = bf16[16,144,256]{2,1,0:T(8,128)(2,1)S(1)} all-to-all(bf16[16,144,256]{2,1,0:T(8,128)(2,1)S(1)} %spread_kernel.1), channel_id=1, replica_groups=mesh['yh'=2,'x'=4,'yl'=2,'yp'=2,'zl'=6,'zp'=2,'core'=2] {'x','yp','zp'}, dimensions={0} | all-to-all | bytes 2359296 | tf_op jit(solution)/shard_map/all_to_all | solution.py:38
  108.0 8.2 %collective-permute-start.3 = (bf16[2304,256]{1,0:T(8,128)(2,1)S(1)}, bf16[2304,256]{1,0:T(8,128)(2,1)S(1)}, u32[]{:S(2)}, u32[]{:S(2)}) collective-permute-start(bf16[2304,256]{1,0:T(8,128)(2,1)S(1)} %bitcast.52), channel_id=1, source_target_pairs={{0,1},{1,0},{2,3},{3,2},{4,5},{5,4},{6,7},{7,6},{8,9},{9,8},{10,11... | collective-permute-start | bytes 3538952 | tf_op jit(solution)/shard_map/ppermute | solution.py:154
  116.2 2.7 %collective-permute-start.1 = (f32[6,256]{1,0:T(8,128)S(1)}, f32[6,256]{1,0:T(8,128)S(1)}, u32[]{:S(2)}, u32[]{:S(2)}) collective-permute-start(f32[6,256]{1,0:T(8,128)S(1)} %convert_reduce_fusion), channel_id=1, source_target_pairs={{0,0},{1,384},{2,24},{3,408},{4,1},{5,385},{6,25},{7,409},{8,2},{9... | collective-permute-start | bytes 18440 | tf_op jit(solution)/shard_map/ppermute | solution.py:149
  119.0 9.4 %collective-permute-done.1 = f32[6,256]{1,0:T(8,128)S(1)} collective-permute-done((f32[6,256]{1,0:T(8,128)S(1)}, f32[6,256]{1,0:T(8,128)S(1)}, u32[]{:S(2)}, u32[]{:S(2)}) %collective-permute-start.1) | collective-permute-done | bytes 6176 | tf_op jit(solution)/shard_map/ppermute | solution.py:149
  128.4 0.6 copy.26
  129.0 0.6 copy.27
  129.6 0.6 copy.28
  130.2 0.0 collective-permute-done.3
  130.2 0.2 broadcast_select_fusion.1
  130.5 0.2 fusion.1
  130.6 1.6 %pad_maximum_fusion = bf16[2,4608,128]{2,1,0:T(8,128)(2,1)} fusion(bf16[1,4608,128]{2,1,0:T(8,128)(2,1)S(1)} %get-tuple-element.16, bf16[1,4608,128]{2,1,0:T(8,128)(2,1)S(1)} %get-tuple-element.15), kind=kLoop, calls=%fused_computation.2 | loop fusion | flops 1179648 | bytes 4718592 | tf_op jit(solution)/shard_map/stack | solution.py:156
  (14 shorter events, 0.1 us)
Async XLA Ops:
  0.6 7.3 %copy-start = (f32[2,6,128]{2,0,1:T(2,128)S(1)}, f32[2,6,128]{2,0,1:T(2,128)}, u32[]{:S(2)}) copy-start(f32[2,6,128]{2,0,1:T(2,128)} %param.7) | copy-start | bytes 18436
  0.6 7.3 %copy-start.1 = (f32[2,6,128]{2,0,1:T(2,128)S(1)}, f32[2,6,128]{2,0,1:T(2,128)}, u32[]{:S(2)}) copy-start(f32[2,6,128]{2,0,1:T(2,128)} %param.8) | copy-start | bytes 18436
  0.7 7.3 %copy-start.2 = (f32[2,6,128]{2,0,1:T(2,128)S(1)}, f32[2,6,128]{2,0,1:T(2,128)}, u32[]{:S(2)}) copy-start(f32[2,6,128]{2,0,1:T(2,128)} %param.9) | copy-start | bytes 18436
  5.3 7.4 %collective-permute-start = (bf16[2304,256]{1,0:T(8,128)(2,1)}, bf16[2304,256]{1,0:T(8,128)(2,1)S(1)}, u32[]{:S(2)}, u32[]{:S(2)}) collective-permute-start(bf16[2304,256]{1,0:T(8,128)(2,1)} %gradient_kernel.3), channel_id=1, source_target_pairs={{0,1},{1,0},{2,3},{3,2},{4,5},{5,4},{6,7},{7,6},{8,9},{9,8},{10,11... | collective-permute-start | bytes 3538952 | tf_op jit(solution)/shard_map/ppermute | solution.py:135
  42.6 26.9 %all-to-all-start.1 = ((bf16[24,6,256]{2,1,0:T(8,128)(2,1)}), bf16[24,6,256]{2,1,0:T(8,128)(2,1)S(1)}, u32[]{:S(2)}, u32[]{:S(2)}) async-start(bf16[24,6,256]{2,1,0:T(8,128)(2,1)} %sum_kernel.1), calls=%async_computation.1 | async-start | bytes 196608 | tf_op jit(solution)/shard_map/all_to_all | solution.py:38
  55.0 14.6 %collective-permute-start.2 = (f32[3,6,256]{2,1,0:T(8,128)S(1)}, f32[3,6,256]{2,1,0:T(8,128)S(1)}, u32[]{:S(2)}, u32[]{:S(2)}) collective-permute-start(f32[3,6,256]{2,1,0:T(8,128)S(1)} %pad_maximum_fusion.2), channel_id=1, source_target_pairs={{0,0},{384,1},{24,2},{408,3},{1,4},{385,5},{25,6},{409,7},{2,8},{3... | collective-permute-start | bytes 55304 | tf_op jit(solution)/shard_map/ppermute | solution.py:141
  108.0 22.3 %collective-permute-start.3 = (bf16[2304,256]{1,0:T(8,128)(2,1)S(1)}, bf16[2304,256]{1,0:T(8,128)(2,1)S(1)}, u32[]{:S(2)}, u32[]{:S(2)}) collective-permute-start(bf16[2304,256]{1,0:T(8,128)(2,1)S(1)} %bitcast.52), channel_id=1, source_target_pairs={{0,1},{1,0},{2,3},{3,2},{4,5},{5,4},{6,7},{7,6},{8,9},{9,8},{10,11... | collective-permute-start | bytes 3538952 | tf_op jit(solution)/shard_map/ppermute | solution.py:154
  116.2 12.2 %collective-permute-start.1 = (f32[6,256]{1,0:T(8,128)S(1)}, f32[6,256]{1,0:T(8,128)S(1)}, u32[]{:S(2)}, u32[]{:S(2)}) collective-permute-start(f32[6,256]{1,0:T(8,128)S(1)} %convert_reduce_fusion), channel_id=1, source_target_pairs={{0,0},{1,384},{2,24},{3,408},{4,1},{5,385},{6,25},{7,409},{8,2},{9... | collective-permute-start | bytes 18440 | tf_op jit(solution)/shard_map/ppermute | solution.py:149

commit v3 on v2

v3 whole, which is shorter than its diff:
```python
import functools

import jax
import jax.numpy as jnp
from jax import lax
from jax.experimental import pallas as pl
from jax.experimental.pallas import tpu as pltpu
from jax.sharding import Mesh
from jax.sharding import PartitionSpec as P

ALL = ("yh", "x", "yl", "yp", "z", "core")
SIZES = (2, 4, 2, 2, 12, 2)
NEAR = ("x", "yp")
FAR = ("yh", "yl", "z")
SWAP = [(0, 1), (1, 0)]
N_NEAR, N_FAR = 8, 48
D, COLS = 4608, 128
ROWS = 12
BLOCK = 144
STEP = 1152

VMEM = pl.BlockSpec(memory_space=pltpu.VMEM)
PARAMS = pltpu.CompilerParams(vmem_limit_bytes=24 * 2**20)
NEAR_BLOCKS = jax.ShapeDtypeStruct((N_NEAR, N_FAR * ROWS, COLS), jnp.bfloat16)


def exchange(blocks, axes):
    return lax.all_to_all(blocks, axes, 0, 0, tiled=True)


def place(block):
    yh, x, yl, yp = block // 16, block // 4 % 4, block // 2 % 2, block % 2
    return x * 2 + yp, (yh * 2 + yl) * BLOCK


def gradient_kernel(other, tokens, cotangents, out):
    core = lax.axis_index("core")
    bucket = 1 - core if other else core
    turned = cotangents[bucket].astype(jnp.float32).T.astype(jnp.bfloat16)
    for step in range(D // STEP):
        product = jnp.dot(
            turned, tokens[:, step * STEP : (step + 1) * STEP], preferred_element_type=jnp.float32
        )
        rows = product.astype(out.dtype).T
        for part in range(STEP // BLOCK):
            chip, first = place(step * (STEP // BLOCK) + part)
            out[chip, first : first + BLOCK, :] = rows[part * BLOCK : (part + 1) * BLOCK, :]


def local_gradient(tokens, cotangents, other):
    count = tokens.shape[0]
    return pl.pallas_call(
        functools.partial(gradient_kernel, other),
        out_shape=NEAR_BLOCKS,
        in_specs=[VMEM, VMEM],
        out_specs=VMEM,
        compiler_params=PARAMS,
        cost_estimate=pl.CostEstimate(
            flops=2 * count * D * COLS, bytes_accessed=count * D * 2, transcendentals=0
        ),
        name="gradient_kernel",
    )(tokens, cotangents)


def add_kernel(left, right, out):
    out[...] = (left[...].astype(jnp.float32) + right[...].astype(jnp.float32)).astype(out.dtype)


def add(left, right):
    return pl.pallas_call(
        add_kernel,
        out_shape=NEAR_BLOCKS,
        in_specs=[VMEM, VMEM],
        out_specs=VMEM,
        compiler_params=PARAMS,
        name="add_kernel",
    )(left, right)


def sum_kernel(blocks, out, held):
    held[...] = blocks[...].astype(jnp.float32).sum(0)
    for index in range(N_FAR):
        out[index] = held[index * ROWS : (index + 1) * ROWS, :].astype(out.dtype)


def sum_near(blocks):
    return pl.pallas_call(
        sum_kernel,
        out_shape=jax.ShapeDtypeStruct((N_FAR, ROWS, COLS), jnp.bfloat16),
        in_specs=[VMEM],
        out_specs=VMEM,
        scratch_shapes=[pltpu.VMEM((N_FAR * ROWS, COLS), jnp.float32)],
        compiler_params=PARAMS,
        name="sum_kernel",
    )(blocks)


def spread_kernel(blocks, out, held):
    for index in range(N_FAR):
        held[index * ROWS : (index + 1) * ROWS, :] = blocks[index].astype(jnp.float32)
    rows = held[...].astype(out.dtype)
    for index in range(N_NEAR):
        out[index] = rows


def spread_far(blocks):
    return pl.pallas_call(
        spread_kernel,
        out_shape=NEAR_BLOCKS,
        in_specs=[VMEM],
        out_specs=VMEM,
        scratch_shapes=[pltpu.VMEM((N_FAR * ROWS, COLS), jnp.float32)],
        compiler_params=PARAMS,
        name="spread_kernel",
    )(blocks)


def write_kernel(other, *refs):
    blocks, out, done = refs[0], refs[-2], refs[-1]
    core = lax.axis_index("core")
    bucket = 1 - core if other else core
    copies = []
    for x in range(4):
        for yp in range(2):
            copies.append(
                pltpu.make_async_copy(
                    blocks.at[x, yp], out.at[bucket, :, x, :, yp], done.at[x * 2 + yp]
                )
            )
            copies[-1].start()
    for copy in copies:
        copy.wait()


def write_bucket(blocks, other, out=None):
    shape = (2, 2, 4, 2, 2, BLOCK, COLS)
    whole = pl.BlockSpec(memory_space=pl.ANY)
    blocks = blocks.reshape(4, 2, 2, 2, BLOCK, COLS)
    return pl.pallas_call(
        functools.partial(write_kernel, other),
        out_shape=jax.ShapeDtypeStruct(shape, jnp.bfloat16),
        in_specs=[VMEM] if out is None else [VMEM, whole],
        out_specs=whole,
        scratch_shapes=[pltpu.SemaphoreType.DMA((N_NEAR,))],
        input_output_aliases={} if out is None else {1: 0},
        compiler_params=PARAMS,
        cost_estimate=pl.CostEstimate(flops=0, bytes_accessed=2 * D * COLS * 2, transcendentals=0),
        name="write_kernel",
    )(*([blocks] if out is None else [blocks, out]))


def adam(gradient, params, moment, second):
    new_moment = 0.9 * moment + 0.1 * gradient
    new_second = 0.95 * second + 0.05 * gradient * gradient
    first_fix = 1.0 - 0.9**10
    second_fix = 1.0 - 0.95**10
    update = new_moment / first_fix / (jnp.sqrt(new_second / second_fix) + 1e-08)
    new_params = params - 0.01 * (update + 0.1 * params)
    return new_params, new_moment, new_second


def in_order(first, home, other, axis):
    return jnp.concatenate([jnp.where(first, home, other), jnp.where(first, other, home)], axis=axis)


def on_device(tokens, cotangents, params, moment, second):
    first = lax.axis_index("core") == 0

    away = lax.ppermute(local_gradient(tokens, cotangents, True), "core", SWAP)
    part = add(local_gradient(tokens, cotangents, False), away)

    state = jnp.stack([params, moment, second], axis=1)
    state, part = lax.optimization_barrier((state, part))
    home_state = jnp.where(first, state[0], state[1])
    other_state = lax.ppermute(jnp.where(first, state[1], state[0]), "core", SWAP)
    held = in_order(first, home_state, other_state, 1)

    near = sum_near(exchange(part, NEAR))
    near, held = lax.optimization_barrier((near, held))
    gradient = exchange(near, FAR).astype(jnp.float32).sum(0)
    rounded = adam(gradient, *held)[0].astype(jnp.bfloat16)
    far = exchange(jnp.broadcast_to(rounded, (N_FAR, ROWS, COLS)), FAR)

    keep = jnp.where(first, gradient[:6], gradient[6:])
    other = lax.ppermute(jnp.where(first, gradient[6:], gradient[:6]), "core", SWAP)
    owned = in_order(first, keep[None], other[None], 0)
    new_params, new_moment, new_second = adam(owned, params, moment, second)
    far, new_params, new_moment, new_second = lax.optimization_barrier(
        (far, new_params, new_moment, new_second)
    )

    mine = exchange(spread_far(far), NEAR)
    theirs = lax.ppermute(mine, "core", SWAP)
    gathered = write_bucket(theirs, True, write_bucket(mine, False))
    return (new_params, new_moment, new_second, gathered.reshape(2, D, COLS))


def solution(mesh):
    fine = Mesh(mesh.devices.reshape(SIZES), ALL)
    rows = P(None, ALL, None)
    return jax.shard_map(
        on_device,
        mesh=fine,
        in_specs=(P(ALL, None), rows, rows, rows, rows),
        out_specs=(rows, rows, rows, P()),
        check_vma=False,
    )
```

time: 133 us -> 124 us (0.932)
  the two profiles are of different devices: /device:TPU:73 before, /device:TPU:1 now
where the time goes in v3:
time: 124 us
  blocking collectives  45.2 us (36%)
  starting transfers between devices  33.7 us (27%)
  waiting for transfers between devices  32.8 us (26%)
  Pallas kernels  5.71 us (5%)
  local copies, waits for them, and re-layouts  5.44 us (4%)
    all_to_all x2, blocking collectives, exchange(): return lax.all_to_all(blocks, axes, 0, 0, tiled=True)  45.2 us
    all_to_all x2, waiting for transfers between devices, exchange(): return lax.all_to_all(blocks, axes, 0, 0, tiled=True)  30.6 us
    ppermute x1, starting transfers between devices, on_device(): away = lax.ppermute(local_gradient(tokens, cotangents, True), 'core', SWAP)  12.4 us
    all_to_all x2, starting transfers between devices, exchange(): return lax.all_to_all(blocks, axes, 0, 0, tiled=True)  8.1 us
    ppermute x1, starting transfers between devices, on_device(): lax.ppermute(jnp.where(first, gradient[6:], gradient[:6]), 'core', SWAP)  5.74 us
    ppermute x1, starting transfers between devices, on_device(): theirs = lax.ppermute(mine, 'core', SWAP)  5.19 us
    unnamed x14, local copies, waits for them, and re-layouts  4.73 us
  transfers between devices with their start and end apart: 6, of which 4 were waited for; matrix products, arithmetic and copies ran while one was open for 2% of the time, Pallas kernels for 2%

profile of v3, /device:TPU:1, one launch (start us, length us, event | category | flops | bytes accessed | tf_op | source)
XLA Modules:
  0.0 123.9 jit_solution(14738858390194748844)
XLA Ops:
  0.6 0.0 copy-start
  0.6 2.0 %copy-done = bf16[384,4608]{1,0:T(8,128)(2,1)S(1)} copy-done((bf16[384,4608]{1,0:T(8,128)(2,1)S(1)}, bf16[384,4608]{1,0:T(8,128)(2,1)}, u32[]{:S(2)}) %copy-start) | copy-done | bytes 3538968
  2.6 0.0 copy-start.1
  2.6 0.9 copy-done.1
  3.6 0.0 copy-start.3
  3.6 1.0 gradient_kernel.3
  4.5 12.4 %collective-permute-start = (bf16[8,576,128]{2,1,0:T(8,128)(2,1)S(1)}, bf16[8,576,128]{2,1,0:T(8,128)(2,1)S(1)}, u32[]{:S(2)}, u32[]{:S(2)}) collective-permute-start(bf16[8,576,128]{2,1,0:T(8,128)(2,1)S(1)} %gradient_kernel.3), channel_id=1, source_target_pairs={{0,1},{1,0},{2,3},{3,2},{4,5},{5,4},{6,7},{7,6},{8,9},{9,8},{10,11... | collective-permute-start | bytes 3538952 | tf_op jit(solution)/shard_map/ppermute | solution.py:169
  17.0 0.0 copy-done.3
  17.0 0.0 copy-start.2
  17.0 0.0 copy-start.4
  17.0 1.0 gradient_kernel.2.left
  18.0 0.0 copy-done.2
  18.0 0.0 copy-done.4
  18.0 1.4 %collective-permute-done.right = bf16[8,576,128]{2,1,0:T(8,128)(2,1)S(1)} collective-permute-done((bf16[8,576,128]{2,1,0:T(8,128)(2,1)S(1)}, bf16[8,576,128]{2,1,0:T(8,128)(2,1)S(1)}, u32[]{:S(2)}, u32[]{:S(2)}) %collective-permute-start) | collective-permute-done | bytes 1179680 | tf_op jit(solution)/shard_map/ppermute | solution.py:169
  19.4 1.3 %add_kernel.1 = bf16[8,576,128]{2,1,0:T(8,128)(2,1)} custom-call(bf16[8,576,128]{2,1,0:T(8,128)(2,1)S(1)} %gradient_kernel.2.left, bf16[8,576,128]{2,1,0:T(8,128)(2,1)S(1)} %collective-permute-done.right), custom_call_target="tpu_custom_call" | custom-call | tf_op jit(solution)/shard_map/add_kernel/pallas_call | solution.py:70
  20.7 3.6 %all-to-all-start = ((bf16[8,576,128]{2,1,0:T(8,128)(2,1)}), bf16[8,576,128]{2,1,0:T(8,128)(2,1)S(1)}, u32[]{:S(2)}, u32[]{:S(2)}) async-start(bf16[8,576,128]{2,1,0:T(8,128)(2,1)} %add_kernel.1), calls=%async_computation | async-start | bytes 2359296 | tf_op jit(solution)/shard_map/all_to_all | solution.py:28
  24.3 2.3 %collective-permute-start.1 = (f32[3,6,128]{2,1,0:T(8,128)S(1)}, f32[3,6,128]{2,1,0:T(8,128)S(1)}, u32[]{:S(2)}, u32[]{:S(2)}) collective-permute-start(f32[3,6,128]{2,1,0:T(8,128)S(1)} %select_bitcast_fusion), channel_id=1, source_target_pairs={{0,1},{1,0},{2,3},{3,2},{4,5},{5,4},{6,7},{7,6},{8,9},{9,8},{10,11... | collective-permute-start | bytes 27656 | tf_op jit(solution)/shard_map/ppermute | solution.py:175
  26.6 0.8 collective-permute-done.1
  27.4 13.7 %all-to-all-done.blocks = bf16[8,576,128]{2,1,0:T(8,128)(2,1)S(1)} async-done(((bf16[8,576,128]{2,1,0:T(8,128)(2,1)}), bf16[8,576,128]{2,1,0:T(8,128)(2,1)S(1)}, u32[]{:S(2)}, u32[]{:S(2)}) %all-to-all-start) | async-done | bytes 1179680 | tf_op jit(solution)/shard_map/all_to_all | solution.py:28
  41.1 0.2 sum_kernel.1
  41.4 27.2 %all_to_all.20 = bf16[48,12,128]{2,1,0:T(8,128)(2,1)S(1)} all-to-all(bf16[48,12,128]{2,1,0:T(8,128)(2,1)S(1)} %sum_kernel.1), channel_id=1, replica_groups=mesh['yh'=2,'x'=4,'yl'=2,'yp'=2,'z'=12,'core'=2] {'yh','yl','z'}, dimensions={0} | all-to-all | bytes 294912 | tf_op jit(solution)/shard_map/all_to_all | solution.py:28
  68.6 0.1 convert_reduce_fusion
  68.7 5.7 %collective-permute-start.2 = (f32[6,128]{1,0:T(8,128)S(1)}, f32[6,128]{1,0:T(8,128)S(1)}, u32[]{:S(2)}, u32[]{:S(2)}) collective-permute-start(f32[6,128]{1,0:T(8,128)S(1)} %slice_select_fusion.1), channel_id=1, source_target_pairs={{0,1},{1,0},{2,3},{3,2},{4,5},{5,4},{6,7},{7,6},{8,9},{9,8},{10,11... | collective-permute-start | bytes 9224 | tf_op jit(solution)/shard_map/ppermute | solution.py:185
  74.4 0.7 broadcast_in_dim.2
  75.1 4.5 %all-to-all-start.2 = ((bf16[48,12,128]{2,1,0:T(8,128)(2,1)}), bf16[48,12,128]{2,1,0:T(8,128)(2,1)S(1)}, u32[]{:S(2)}, u32[]{:S(2)}) async-start(bf16[48,12,128]{2,1,0:T(8,128)(2,1)} %broadcast_in_dim.2), calls=%async_computation.2 | async-start | bytes 393216 | tf_op jit(solution)/shard_map/all_to_all | solution.py:28
  79.7 0.0 collective-permute-done.2
  79.7 16.9 %all-to-all-done.2.blocks = bf16[48,12,128]{2,1,0:T(8,128)(2,1)S(1)} async-done(((bf16[48,12,128]{2,1,0:T(8,128)(2,1)}), bf16[48,12,128]{2,1,0:T(8,128)(2,1)S(1)}, u32[]{:S(2)}, u32[]{:S(2)}) %all-to-all-start.2) | async-done | bytes 147488 | tf_op jit(solution)/shard_map/all_to_all | solution.py:28
  96.6 0.1 spread_kernel.1
  96.7 18.0 %all_to_all.21 = bf16[8,576,128]{2,1,0:T(8,128)(2,1)S(1)} all-to-all(bf16[8,576,128]{2,1,0:T(8,128)(2,1)S(1)} %spread_kernel.1), channel_id=1, replica_groups=mesh['yh'=2,'x'=4,'yl'=2,'yp'=2,'z'=12,'core'=2] {'x','yp'}, dimensions={0} | all-to-all | bytes 2359296 | tf_op jit(solution)/shard_map/all_to_all | solution.py:28
  114.7 5.2 %collective-permute-start.3 = (bf16[8,576,128]{2,1,0:T(8,128)(2,1)S(1)}, bf16[8,576,128]{2,1,0:T(8,128)(2,1)S(1)}, u32[]{:S(2)}, u32[]{:S(2)}) collective-permute-start(bf16[8,576,128]{2,1,0:T(8,128)(2,1)S(1)} %all_to_all.21), channel_id=1, source_target_pairs={{0,1},{1,0},{2,3},{3,2},{4,5},{5,4},{6,7},{7,6},{8,9},{9,8},{10,11... | collective-permute-start | bytes 3538952 | tf_op jit(solution)/shard_map/ppermute | solution.py:193
  119.9 0.6 copy.21
  120.5 0.6 copy.22
  121.1 0.6 copy.23
  121.7 1.1 write_kernel.2.refs_1_
  122.8 0.0 collective-permute-done.3
  122.8 1.1 write_kernel.3
  (10 shorter events, 0.1 us)
Async XLA Ops:
  0.6 2.0 %copy-start = (bf16[384,4608]{1,0:T(8,128)(2,1)S(1)}, bf16[384,4608]{1,0:T(8,128)(2,1)}, u32[]{:S(2)}) copy-start(bf16[384,4608]{1,0:T(8,128)(2,1)} %tokens.3) | copy-start | bytes 10616836
  2.6 0.9 copy-start.1
  3.6 13.4 %copy-start.3 = (f32[2,6,128]{2,0,1:T(2,128)S(1)}, f32[2,6,128]{2,0,1:T(2,128)}, u32[]{:S(2)}) copy-start(f32[2,6,128]{2,0,1:T(2,128)} %param.8) | copy-start | bytes 18436
  4.5 14.9 %collective-permute-start = (bf16[8,576,128]{2,1,0:T(8,128)(2,1)S(1)}, bf16[8,576,128]{2,1,0:T(8,128)(2,1)S(1)}, u32[]{:S(2)}, u32[]{:S(2)}) collective-permute-start(bf16[8,576,128]{2,1,0:T(8,128)(2,1)S(1)} %gradient_kernel.3), channel_id=1, source_target_pairs={{0,1},{1,0},{2,3},{3,2},{4,5},{5,4},{6,7},{7,6},{8,9},{9,8},{10,11... | collective-permute-start | bytes 3538952 | tf_op jit(solution)/shard_map/ppermute | solution.py:169
  17.0 1.0 copy-start.2
  17.0 1.0 copy-start.4
  20.7 20.4 %all-to-all-start = ((bf16[8,576,128]{2,1,0:T(8,128)(2,1)}), bf16[8,576,128]{2,1,0:T(8,128)(2,1)S(1)}, u32[]{:S(2)}, u32[]{:S(2)}) async-start(bf16[8,576,128]{2,1,0:T(8,128)(2,1)} %add_kernel.1), calls=%async_computation | async-start | bytes 2359296 | tf_op jit(solution)/shard_map/all_to_all | solution.py:28
  24.3 3.1 %collective-permute-start.1 = (f32[3,6,128]{2,1,0:T(8,128)S(1)}, f32[3,6,128]{2,1,0:T(8,128)S(1)}, u32[]{:S(2)}, u32[]{:S(2)}) collective-permute-start(f32[3,6,128]{2,1,0:T(8,128)S(1)} %select_bitcast_fusion), channel_id=1, source_target_pairs={{0,1},{1,0},{2,3},{3,2},{4,5},{5,4},{6,7},{7,6},{8,9},{9,8},{10,11... | collective-permute-start | bytes 27656 | tf_op jit(solution)/shard_map/ppermute | solution.py:175
  68.7 11.0 %collective-permute-start.2 = (f32[6,128]{1,0:T(8,128)S(1)}, f32[6,128]{1,0:T(8,128)S(1)}, u32[]{:S(2)}, u32[]{:S(2)}) collective-permute-start(f32[6,128]{1,0:T(8,128)S(1)} %slice_select_fusion.1), channel_id=1, source_target_pairs={{0,1},{1,0},{2,3},{3,2},{4,5},{5,4},{6,7},{7,6},{8,9},{9,8},{10,11... | collective-permute-start | bytes 9224 | tf_op jit(solution)/shard_map/ppermute | solution.py:185
  75.1 21.4 %all-to-all-start.2 = ((bf16[48,12,128]{2,1,0:T(8,128)(2,1)}), bf16[48,12,128]{2,1,0:T(8,128)(2,1)S(1)}, u32[]{:S(2)}, u32[]{:S(2)}) async-start(bf16[48,12,128]{2,1,0:T(8,128)(2,1)} %broadcast_in_dim.2), calls=%async_computation.2 | async-start | bytes 393216 | tf_op jit(solution)/shard_map/all_to_all | solution.py:28
  114.7 8.1 %collective-permute-start.3 = (bf16[8,576,128]{2,1,0:T(8,128)(2,1)S(1)}, bf16[8,576,128]{2,1,0:T(8,128)(2,1)S(1)}, u32[]{:S(2)}, u32[]{:S(2)}) collective-permute-start(bf16[8,576,128]{2,1,0:T(8,128)(2,1)S(1)} %all_to_all.21), channel_id=1, source_target_pairs={{0,1},{1,0},{2,3},{3,2},{4,5},{5,4},{6,7},{7,6},{8,9},{9,8},{10,11... | collective-permute-start | bytes 3538952 | tf_op jit(solution)/shard_map/ppermute | solution.py:193

commit v4 on v3

--- a/solution.py
+++ b/solution.py
@@ -21,7 +21,8 @@
 
 VMEM = pl.BlockSpec(memory_space=pltpu.VMEM)
 PARAMS = pltpu.CompilerParams(vmem_limit_bytes=24 * 2**20)
-NEAR_BLOCKS = jax.ShapeDtypeStruct((N_NEAR, N_FAR * ROWS, COLS), jnp.bfloat16)
+NEAR_BLOCKS = pltpu.VMEM((N_NEAR, N_FAR * ROWS, COLS), jnp.bfloat16)
+FAR_BLOCKS = pltpu.VMEM((N_FAR, ROWS, COLS), jnp.bfloat16)
 
 
 def exchange(blocks, axes):
@@ -33,11 +34,9 @@
     return x * 2 + yp, (yh * 2 + yl) * BLOCK
 
 
-def gradient_kernel(other, tokens, cotangents, out):
-    core = lax.axis_index("core")
-    bucket = 1 - core if other else core
-    turned = cotangents[bucket].astype(jnp.float32).T.astype(jnp.bfloat16)
-    for step in range(D // STEP):
+def multiply(tokens, cotangent, out, columns):
+    turned = cotangent.astype(jnp.float32).T.astype(jnp.bfloat16)
+    for step in columns:
         product = jnp.dot(
             turned, tokens[:, step * STEP : (step + 1) * STEP], preferred_element_type=jnp.float32
         )
@@ -47,18 +46,55 @@
             out[chip, first : first + BLOCK, :] = rows[part * BLOCK : (part + 1) * BLOCK, :]
 
 
-def local_gradient(tokens, cotangents, other):
-    count = tokens.shape[0]
-    return pl.pallas_call(
-        functools.partial(gradient_kernel, other),
+def first_kernel(tokens, cotangents, out, held, small, arrived):
+    other = 1 - lax.axis_index("core")
+    copies = [pltpu.make_async_copy(cotangents, small, arrived.at[2])]
+    for half in range(2):
+        columns = (slice(None), pl.ds(half * (D // 2), D // 2))
+        copies.append(
+            pltpu.make_async_copy(tokens.at[columns], held.at[columns], arrived.at[half])
+        )
+    for copy in copies:
+        copy.start()
+    copies[0].wait()
+    for half in range(2):
+        copies[1 + half].wait()
+        multiply(held, small[other], out, (2 * half, 2 * half + 1))
+
+
+def second_kernel(tokens, cotangents, out):
+    multiply(tokens, cotangents[lax.axis_index("core")], out, range(D // STEP))
+
+
+def first_gradient(tokens, cotangents):
+    return pl.pallas_call(
+        first_kernel,
+        out_shape=[
+            NEAR_BLOCKS,
+            pltpu.VMEM(tokens.shape, jnp.bfloat16),
+            pltpu.VMEM(cotangents.shape, jnp.bfloat16),
+        ],
+        in_specs=[pl.BlockSpec(memory_space=pltpu.HBM)] * 2,
+        out_specs=[VMEM] * 3,
+        scratch_shapes=[pltpu.SemaphoreType.DMA((3,))],
+        compiler_params=pltpu.CompilerParams(vmem_limit_bytes=55_000_000),
+        name="first_kernel",
+    )(tokens, cotangents)
+
+
+def second_gradient(tokens, cotangents):
+    return pl.pallas_call(
+        second_kernel,
         out_shape=NEAR_BLOCKS,
         in_specs=[VMEM, VMEM],
         out_specs=VMEM,
         compiler_params=PARAMS,
         cost_estimate=pl.CostEstimate(
-            flops=2 * count * D * COLS, bytes_accessed=count * D * 2, transcendentals=0
+            flops=2 * tokens.shape[0] * D * COLS,
+            bytes_accessed=tokens.size * 2,
+            transcendentals=0,
         ),
-        name="gradient_kernel",
+        name="second_kernel",
     )(tokens, cotangents)
 
 
@@ -86,7 +122,7 @@
 def sum_near(blocks):
     return pl.pallas_call(
         sum_kernel,
-        out_shape=jax.ShapeDtypeStruct((N_FAR, ROWS, COLS), jnp.bfloat16),
+        out_shape=FAR_BLOCKS,
         in_specs=[VMEM],
         out_specs=VMEM,
         scratch_shapes=[pltpu.VMEM((N_FAR * ROWS, COLS), jnp.float32)],
@@ -159,6 +195,24 @@
     return new_params, new_moment, new_second
 
 
+def finish_kernel(blocks, state, gradient, out):
+    gradient[...] = blocks[...].astype(jnp.float32).sum(0)
+    rounded = adam(gradient[...], state[0], state[1], state[2])[0].astype(out.dtype)
+    for index in range(N_FAR):
+        out[index] = rounded
+
+
+def finish(blocks, state):
+    return pl.pallas_call(
+        finish_kernel,
+        out_shape=[pltpu.VMEM((ROWS, COLS), jnp.float32), FAR_BLOCKS],
+        in_specs=[VMEM, VMEM],
+        out_specs=[VMEM, VMEM],
+        compiler_params=PARAMS,
+        name="finish_kernel",
+    )(blocks, state)
+
+
 def in_order(first, home, other, axis):
     return jnp.concatenate([jnp.where(first, home, other), jnp.where(first, other, home)], axis=axis)
 
@@ -166,20 +220,20 @@
 def on_device(tokens, cotangents, params, moment, second):
     first = lax.axis_index("core") == 0
 
-    away = lax.ppermute(local_gradient(tokens, cotangents, True), "core", SWAP)
-    part = add(local_gradient(tokens, cotangents, False), away)
+    away, tokens, cotangents = first_gradient(tokens, cotangents)
+    away = lax.ppermute(away, "core", SWAP)
+    home = second_gradient(tokens, cotangents)
 
     state = jnp.stack([params, moment, second], axis=1)
-    state, part = lax.optimization_barrier((state, part))
+    state, home = lax.optimization_barrier((state, home))
     home_state = jnp.where(first, state[0], state[1])
     other_state = lax.ppermute(jnp.where(first, state[1], state[0]), "core", SWAP)
     held = in_order(first, home_state, other_state, 1)
-
-    near = sum_near(exchange(part, NEAR))
-    near, held = lax.optimization_barrier((near, held))
-    gradient = exchange(near, FAR).astype(jnp.float32).sum(0)
-    rounded = adam(gradient, *held)[0].astype(jnp.bfloat16)
-    far = exchange(jnp.broadcast_to(rounded, (N_FAR, ROWS, COLS)), FAR)
+    away, held = lax.optimization_barrier((away, held))
+
+    near = sum_near(exchange(add(home, away), NEAR))
+    gradient, rounded = finish(exchange(near, FAR), held)
+    far = exchange(rounded, FAR)
 
     keep = jnp.where(first, gradient[:6], gradient[6:])
     other = lax.ppermute(jnp.where(first, gradient[6:], gradient[:6]), "core", SWAP)

time: 124 us -> 126 us (1.016)
  blocking collectives: 45.2 us -> 64.9 us
  waiting for transfers between devices: 32.8 us -> 18 us
  starting transfers between devices: 33.7 us -> 29.8 us
  local copies, waits for them, and re-layouts: 5.44 us -> 1.82 us
  other arithmetic: 0.14 us -> 2.11 us
  Pallas kernels: 5.71 us -> 7.37 us
    all_to_all x2 -> x3, blocking collectives: 45.2 us -> 64.9 us  [exchange(): return lax.all_to_all(blocks, axes, 0, 0, tiled=True)]
    all_to_all x2 -> x1, waiting for transfers between devices: 30.6 us -> 16.8 us  [exchange(): return lax.all_to_all(blocks, axes, 0, 0, tiled=True)]
    all_to_all x2 -> x1, starting transfers between devices: 8.1 us -> 4.54 us  [exchange(): return lax.all_to_all(blocks, axes, 0, 0, tiled=True)]
    unnamed x14 -> x12, local copies, waits for them, and re-layouts: 4.73 us -> 1.82 us
    pallas_call x3 -> x4, Pallas kernels: 2.17 us -> 4.85 us  [the longest x1 2.85 us: first_gradient(): pl.pallas_call(first_kernel, out_shape=[NEAR_BLOCKS, pltpu.VMEM(tokens.sh...]
    ppermute x1, waiting for transfers between devices: 1.39 us -> 0.01 us  [on_device(): away = lax.ppermute(away, 'core', SWAP)]
  transfers between devices with their start and end apart: 6 -> 5, of which waited for: 4 -> 2; matrix products, arithmetic and copies ran while one was open for 2% -> 3% of each run, Pallas kernels for 2% -> 2%
where the time goes in v4:
time: 126 us; the launch traced here: 125 us
  blocking collectives  64.9 us (52%)
  starting transfers between devices  29.8 us (24%)
  waiting for transfers between devices  18 us (14%)
  Pallas kernels  7.37 us (6%)
  other arithmetic  2.11 us (2%)
  local copies, waits for them, and re-layouts  1.82 us (1%)
    all_to_all x3, blocking collectives, exchange(): return lax.all_to_all(blocks, axes, 0, 0, tiled=True)  64.9 us
    all_to_all x1, waiting for transfers between devices, exchange(): return lax.all_to_all(blocks, axes, 0, 0, tiled=True)  16.8 us
    ppermute x1, starting transfers between devices, on_device(): away = lax.ppermute(away, 'core', SWAP)  12.4 us
    ppermute x1, starting transfers between devices, on_device(): lax.ppermute(jnp.where(first, gradient[6:], gradient[:6]), 'core', SWAP)  5.74 us
    ppermute x1, starting transfers between devices, on_device(): theirs = lax.ppermute(mine, 'core', SWAP)  5.16 us
    all_to_all x1, starting transfers between devices, exchange(): return lax.all_to_all(blocks, axes, 0, 0, tiled=True)  4.54 us
    pallas_call x1, Pallas kernels, first_gradient(): pl.pallas_call(first_kernel, out_shape=[NEAR_BLOCKS, pltpu.VMEM(tokens.sh...  2.85 us
  transfers between devices with their start and end apart: 5, of which 2 were waited for; matrix products, arithmetic and copies ran while one was open for 3% of the time, Pallas kernels for 2%

profile of v4, /device:TPU:1, one launch (start us, length us, event | category | flops | bytes accessed | tf_op | source)
XLA Modules:
  0.0 124.8 jit_solution(17663686354552833287)
XLA Ops:
  0.6 0.0 copy-start.2
  0.6 2.9 %first_kernel.1 = (bf16[8,576,128]{2,1,0:T(8,128)(2,1)S(1)}, bf16[384,4608]{1,0:T(8,128)(2,1)S(1)}, bf16[2,384,128]{2,1,0:T(8,128)(2,1)S(1)}) custom-call(bf16[384,4608]{1,0:T(8,128)(2,1)} %tokens.1, bf16[2,384,128]{2,1,0:T(8,128)(2,1)} %cotangents.1), custom_call_target="tpu_custom_call" | custom-call | tf_op jit(solution)/shard_map/first_kernel/pallas_call | solution.py:70
  3.5 12.4 %collective-permute-start = (bf16[8,576,128]{2,1,0:T(8,128)(2,1)S(1)}, bf16[8,576,128]{2,1,0:T(8,128)(2,1)S(1)}, u32[]{:S(2)}, u32[]{:S(2)}) collective-permute-start(bf16[8,576,128]{2,1,0:T(8,128)(2,1)S(1)} %get-tuple-element.20), channel_id=1, source_target_pairs={{0,1},{1,0},{2,3},{3,2},{4,5},{5,4},{6,7},{7,6},{8,9},{9,8},{10,11... | collective-permute-start | bytes 3538952 | tf_op jit(solution)/shard_map/ppermute | solution.py:224
  15.9 0.0 copy-done.2
  16.0 0.0 copy-start
  16.0 0.0 copy-start.1
  16.0 1.0 second_kernel.1.left
  17.0 0.0 copy-done
  17.0 0.0 copy-done.1
  17.0 0.6 pad_maximum_fusion
  17.6 0.7 select_bitcast_fusion
  18.3 1.9 %collective-permute-start.1 = (f32[3,6,128]{2,1,0:T(8,128)S(1)}, f32[3,6,128]{2,1,0:T(8,128)S(1)}, u32[]{:S(2)}, u32[]{:S(2)}) collective-permute-start(f32[3,6,128]{2,1,0:T(8,128)S(1)} %select_bitcast_fusion), channel_id=1, source_target_pairs={{0,1},{1,0},{2,3},{3,2},{4,5},{5,4},{6,7},{7,6},{8,9},{9,8},{10,11... | collective-permute-start | bytes 27656 | tf_op jit(solution)/shard_map/ppermute | solution.py:230
  20.3 1.1 collective-permute-done.1
  21.4 0.7 bitcast_select_fusion.1
  22.2 0.0 collective-permute-done.right
  22.2 0.3 add_kernel.1
  22.4 19.2 %all_to_all.20.blocks = bf16[8,576,128]{2,1,0:T(8,128)(2,1)S(1)} all-to-all(bf16[8,576,128]{2,1,0:T(8,128)(2,1)S(1)} %add_kernel.1), channel_id=1, replica_groups=mesh['yh'=2,'x'=4,'yl'=2,'yp'=2,'z'=12,'core'=2] {'x','yp'}, dimensions={0} | all-to-all | bytes 2359296 | tf_op jit(solution)/shard_map/all_to_all | solution.py:29
  41.7 0.0 copy-start.3
  41.7 0.2 sum_kernel.1
  41.9 28.4 %all_to_all.21.blocks = bf16[48,12,128]{2,1,0:T(8,128)(2,1)S(1)} all-to-all(bf16[48,12,128]{2,1,0:T(8,128)(2,1)S(1)} %sum_kernel.1), channel_id=1, replica_groups=mesh['yh'=2,'x'=4,'yl'=2,'yp'=2,'z'=12,'core'=2] {'yh','yl','z'}, dimensions={0} | all-to-all | bytes 294912 | tf_op jit(solution)/shard_map/all_to_all | solution.py:29
  70.3 0.8 finish_kernel.1
  71.1 5.7 %collective-permute-start.2 = (f32[6,128]{1,0:T(8,128)S(1)}, f32[6,128]{1,0:T(8,128)S(1)}, u32[]{:S(2)}, u32[]{:S(2)}) collective-permute-start(f32[6,128]{1,0:T(8,128)S(1)} %slice_select_fusion.1), channel_id=1, source_target_pairs={{0,1},{1,0},{2,3},{3,2},{4,5},{5,4},{6,7},{7,6},{8,9},{9,8},{10,11... | collective-permute-start | bytes 9224 | tf_op jit(solution)/shard_map/ppermute | solution.py:239
  76.8 4.5 %all-to-all-start.2 = ((bf16[48,12,128]{2,1,0:T(8,128)(2,1)}), bf16[48,12,128]{2,1,0:T(8,128)(2,1)S(1)}, u32[]{:S(2)}, u32[]{:S(2)}) async-start(bf16[48,12,128]{2,1,0:T(8,128)(2,1)} %get-tuple-element.24), calls=%async_computation.2 | async-start | bytes 393216 | tf_op jit(solution)/shard_map/all_to_all | solution.py:29
  81.4 0.0 collective-permute-done.2
  81.4 0.0 copy-done.3
  81.4 16.8 %all-to-all-done.2.blocks = bf16[48,12,128]{2,1,0:T(8,128)(2,1)S(1)} async-done(((bf16[48,12,128]{2,1,0:T(8,128)(2,1)}), bf16[48,12,128]{2,1,0:T(8,128)(2,1)S(1)}, u32[]{:S(2)}, u32[]{:S(2)}) %all-to-all-start.2) | async-done | bytes 147488 | tf_op jit(solution)/shard_map/all_to_all | solution.py:29
  98.3 0.1 spread_kernel.1
  98.4 17.3 %all_to_all.22 = bf16[8,576,128]{2,1,0:T(8,128)(2,1)S(1)} all-to-all(bf16[8,576,128]{2,1,0:T(8,128)(2,1)S(1)} %spread_kernel.1), channel_id=1, replica_groups=mesh['yh'=2,'x'=4,'yl'=2,'yp'=2,'z'=12,'core'=2] {'x','yp'}, dimensions={0} | all-to-all | bytes 2359296 | tf_op jit(solution)/shard_map/all_to_all | solution.py:29
  115.7 5.2 %collective-permute-start.3 = (bf16[8,576,128]{2,1,0:T(8,128)(2,1)S(1)}, bf16[8,576,128]{2,1,0:T(8,128)(2,1)S(1)}, u32[]{:S(2)}, u32[]{:S(2)}) collective-permute-start(bf16[8,576,128]{2,1,0:T(8,128)(2,1)S(1)} %all_to_all.22), channel_id=1, source_target_pairs={{0,1},{1,0},{2,3},{3,2},{4,5},{5,4},{6,7},{7,6},{8,9},{9,8},{10,11... | collective-permute-start | bytes 3538952 | tf_op jit(solution)/shard_map/ppermute | solution.py:247
  120.9 0.6 copy.17
  121.5 0.6 copy.18
  122.1 0.6 copy.19
  122.7 1.1 write_kernel.2.refs_1_
  123.7 0.0 collective-permute-done.3
  123.8 1.1 write_kernel.3
  (6 shorter events, 0.1 us)
Async XLA Ops:
  0.6 15.3 %copy-start.2 = (f32[2,6,128]{2,0,1:T(2,128)S(1)}, f32[2,6,128]{2,0,1:T(2,128)}, u32[]{:S(2)}) copy-start(f32[2,6,128]{2,0,1:T(2,128)} %param.8) | copy-start | bytes 18436
  3.5 18.7 %collective-permute-start = (bf16[8,576,128]{2,1,0:T(8,128)(2,1)S(1)}, bf16[8,576,128]{2,1,0:T(8,128)(2,1)S(1)}, u32[]{:S(2)}, u32[]{:S(2)}) collective-permute-start(bf16[8,576,128]{2,1,0:T(8,128)(2,1)S(1)} %get-tuple-element.20), channel_id=1, source_target_pairs={{0,1},{1,0},{2,3},{3,2},{4,5},{5,4},{6,7},{7,6},{8,9},{9,8},{10,11... | collective-permute-start | bytes 3538952 | tf_op jit(solution)/shard_map/ppermute | solution.py:224
  16.0 1.0 copy-start
  16.0 1.0 copy-start.1
  18.3 3.1 %collective-permute-start.1 = (f32[3,6,128]{2,1,0:T(8,128)S(1)}, f32[3,6,128]{2,1,0:T(8,128)S(1)}, u32[]{:S(2)}, u32[]{:S(2)}) collective-permute-start(f32[3,6,128]{2,1,0:T(8,128)S(1)} %select_bitcast_fusion), channel_id=1, source_target_pairs={{0,1},{1,0},{2,3},{3,2},{4,5},{5,4},{6,7},{7,6},{8,9},{9,8},{10,11... | collective-permute-start | bytes 27656 | tf_op jit(solution)/shard_map/ppermute | solution.py:230
  41.7 39.7 %copy-start.3 = (f32[2,6,128]{2,0,1:T(2,128)S(1)}, f32[2,6,128]{2,0,1:T(2,128)}, u32[]{:S(2)}) copy-start(f32[2,6,128]{2,0,1:T(2,128)} %param.8) | copy-start | bytes 18436
  71.1 10.3 %collective-permute-start.2 = (f32[6,128]{1,0:T(8,128)S(1)}, f32[6,128]{1,0:T(8,128)S(1)}, u32[]{:S(2)}, u32[]{:S(2)}) collective-permute-start(f32[6,128]{1,0:T(8,128)S(1)} %slice_select_fusion.1), channel_id=1, source_target_pairs={{0,1},{1,0},{2,3},{3,2},{4,5},{5,4},{6,7},{7,6},{8,9},{9,8},{10,11... | collective-permute-start | bytes 9224 | tf_op jit(solution)/shard_map/ppermute | solution.py:239
  76.8 21.5 %all-to-all-start.2 = ((bf16[48,12,128]{2,1,0:T(8,128)(2,1)}), bf16[48,12,128]{2,1,0:T(8,128)(2,1)S(1)}, u32[]{:S(2)}, u32[]{:S(2)}) async-start(bf16[48,12,128]{2,1,0:T(8,128)(2,1)} %get-tuple-element.24), calls=%async_computation.2 | async-start | bytes 393216 | tf_op jit(solution)/shard_map/all_to_all | solution.py:29
  115.7 8.0 %collective-permute-start.3 = (bf16[8,576,128]{2,1,0:T(8,128)(2,1)S(1)}, bf16[8,576,128]{2,1,0:T(8,128)(2,1)S(1)}, u32[]{:S(2)}, u32[]{:S(2)}) collective-permute-start(bf16[8,576,128]{2,1,0:T(8,128)(2,1)S(1)} %all_to_all.22), channel_id=1, source_target_pairs={{0,1},{1,0},{2,3},{3,2},{4,5},{5,4},{6,7},{7,6},{8,9},{9,8},{10,11... | collective-permute-start | bytes 3538952 | tf_op jit(solution)/shard_map/ppermute | solution.py:247

commit v5 on v4

--- a/solution.py
+++ b/solution.py
@@ -222,29 +222,26 @@
 
     away, tokens, cotangents = first_gradient(tokens, cotangents)
     away = lax.ppermute(away, "core", SWAP)
-    home = second_gradient(tokens, cotangents)
-
+    near = sum_near(exchange(add(second_gradient(tokens, cotangents), away), NEAR))
+
+    params, moment, second, near = lax.optimization_barrier((params, moment, second, near))
     state = jnp.stack([params, moment, second], axis=1)
-    state, home = lax.optimization_barrier((state, home))
     home_state = jnp.where(first, state[0], state[1])
     other_state = lax.ppermute(jnp.where(first, state[1], state[0]), "core", SWAP)
     held = in_order(first, home_state, other_state, 1)
-    away, held = lax.optimization_barrier((away, held))
-
-    near = sum_near(exchange(add(home, away), NEAR))
+
     gradient, rounded = finish(exchange(near, FAR), held)
     far = exchange(rounded, FAR)
 
     keep = jnp.where(first, gradient[:6], gradient[6:])
     other = lax.ppermute(jnp.where(first, gradient[6:], gradient[:6]), "core", SWAP)
+    near, other = lax.optimization_barrier((spread_far(far), other))
+
+    mine = exchange(near, NEAR)
+    mine, other = lax.optimization_barrier((mine, other))
+    theirs = lax.ppermute(mine, "core", SWAP)
     owned = in_order(first, keep[None], other[None], 0)
     new_params, new_moment, new_second = adam(owned, params, moment, second)
-    far, new_params, new_moment, new_second = lax.optimization_barrier(
-        (far, new_params, new_moment, new_second)
-    )
-
-    mine = exchange(spread_far(far), NEAR)
-    theirs = lax.ppermute(mine, "core", SWAP)
     gathered = write_bucket(theirs, True, write_bucket(mine, False))
     return (new_params, new_moment, new_second, gathered.reshape(2, D, COLS))
 

time: 126 us -> 119 us (0.944)
  blocking collectives: 64.9 us -> 17 us
  waiting for transfers between devices: 18 us -> 40.5 us
  starting transfers between devices: 29.8 us -> 49.4 us
  other arithmetic: 2.11 us -> 0.06 us
  Pallas kernels: 7.37 us -> 9.04 us
    all_to_all x3 -> x1, blocking collectives: 64.9 us -> 17 us  [exchange(): return lax.all_to_all(blocks, axes, 0, 0, tiled=True)]
    all_to_all x1 -> x3, waiting for transfers between devices: 16.8 us -> 38.2 us  [exchange(): return lax.all_to_all(blocks, axes, 0, 0, tiled=True)]
    all_to_all x1 -> x3, starting transfers between devices: 4.54 us -> 21.4 us  [exchange(): return lax.all_to_all(blocks, axes, 0, 0, tiled=True)]
    ppermute x1, starting transfers between devices: 5.16 us -> 7.35 us  [on_device(): theirs = lax.ppermute(mine, 'core', SWAP)]
    ppermute x1, starting transfers between devices: 1.91 us -> 3.71 us  [on_device(): lax.ppermute(jnp.where(first, state[1], state[0]), 'core', SWAP)]
    ppermute x1, waiting for transfers between devices: 0.01 us -> 1.48 us  [on_device(): away = lax.ppermute(away, 'core', SWAP)]
  transfers between devices with their start and end apart: 5 -> 7, of which waited for: 2 -> 5; matrix products, arithmetic and copies ran while one was open for 3% -> 2% of each run, Pallas kernels for 2% -> 2%
where the time goes in v5:
time: 119 us
  starting transfers between devices  49.4 us (42%)
  waiting for transfers between devices  40.5 us (34%)
  blocking collectives  17 us (14%)
  Pallas kernels  9.04 us (8%)
  local copies, waits for them, and re-layouts  1.82 us (2%)
    all_to_all x3, waiting for transfers between devices, exchange(): return lax.all_to_all(blocks, axes, 0, 0, tiled=True)  38.2 us
    all_to_all x3, starting transfers between devices, exchange(): return lax.all_to_all(blocks, axes, 0, 0, tiled=True)  21.4 us
    all_to_all x1, blocking collectives, exchange(): return lax.all_to_all(blocks, axes, 0, 0, tiled=True)  17 us
    ppermute x1, starting transfers between devices, on_device(): away = lax.ppermute(away, 'core', SWAP)  12.4 us
    ppermute x1, starting transfers between devices, on_device(): theirs = lax.ppermute(mine, 'core', SWAP)  7.35 us
    ppermute x1, starting transfers between devices, on_device(): lax.ppermute(jnp.where(first, gradient[6:], gradient[:6]), 'core', SWAP)  4.55 us
    ppermute x1, starting transfers between devices, on_device(): lax.ppermute(jnp.where(first, state[1], state[0]), 'core', SWAP)  3.71 us
    pallas_call x1, Pallas kernels, first_gradient(): pl.pallas_call(first_kernel, out_shape=[NEAR_BLOCKS, pltpu.VMEM(tokens.sh...  2.85 us
  transfers between devices with their start and end apart: 7, of which 5 were waited for; matrix products, arithmetic and copies ran while one was open for 2% of the time, Pallas kernels for 2%

profile of v5, /device:TPU:1, one launch (start us, length us, event | category | flops | bytes accessed | tf_op | source)
XLA Modules:
  0.0 118.7 jit_solution(1583280294411279640)
XLA Ops:
  0.6 2.8 %first_kernel.1 = (bf16[8,576,128]{2,1,0:T(8,128)(2,1)S(1)}, bf16[384,4608]{1,0:T(8,128)(2,1)S(1)}, bf16[2,384,128]{2,1,0:T(8,128)(2,1)S(1)}) custom-call(bf16[384,4608]{1,0:T(8,128)(2,1)} %tokens.1, bf16[2,384,128]{2,1,0:T(8,128)(2,1)} %cotangents.1), custom_call_target="tpu_custom_call" | custom-call | tf_op jit(solution)/shard_map/first_kernel/pallas_call | solution.py:70
  3.5 12.4 %collective-permute-start = (bf16[8,576,128]{2,1,0:T(8,128)(2,1)S(1)}, bf16[8,576,128]{2,1,0:T(8,128)(2,1)S(1)}, u32[]{:S(2)}, u32[]{:S(2)}) collective-permute-start(bf16[8,576,128]{2,1,0:T(8,128)(2,1)S(1)} %get-tuple-element.19), channel_id=1, source_target_pairs={{0,1},{1,0},{2,3},{3,2},{4,5},{5,4},{6,7},{7,6},{8,9},{9,8},{10,11... | collective-permute-start | bytes 3538952 | tf_op jit(solution)/shard_map/ppermute | solution.py:224
  15.9 1.0 second_kernel.1.left
  16.9 1.5 %collective-permute-done.right = bf16[8,576,128]{2,1,0:T(8,128)(2,1)S(1)} collective-permute-done((bf16[8,576,128]{2,1,0:T(8,128)(2,1)S(1)}, bf16[8,576,128]{2,1,0:T(8,128)(2,1)S(1)}, u32[]{:S(2)}, u32[]{:S(2)}) %collective-permute-start) | collective-permute-done | bytes 1179680 | tf_op jit(solution)/shard_map/ppermute | solution.py:224
  18.4 1.3 %add_kernel.1 = bf16[8,576,128]{2,1,0:T(8,128)(2,1)} custom-call(bf16[8,576,128]{2,1,0:T(8,128)(2,1)S(1)} %second_kernel.1.left, bf16[8,576,128]{2,1,0:T(8,128)(2,1)S(1)} %collective-permute-done.right), custom_call_target="tpu_custom_call" | custom-call | tf_op jit(solution)/shard_map/add_kernel/pallas_call | solution.py:106
  19.7 3.6 %all-to-all-start = ((bf16[8,576,128]{2,1,0:T(8,128)(2,1)}), bf16[8,576,128]{2,1,0:T(8,128)(2,1)S(1)}, u32[]{:S(2)}, u32[]{:S(2)}) async-start(bf16[8,576,128]{2,1,0:T(8,128)(2,1)} %add_kernel.1), calls=%async_computation | async-start | bytes 2359296 | tf_op jit(solution)/shard_map/all_to_all | solution.py:29
  23.2 0.0 copy-start.2
  23.2 0.0 copy-start
  23.3 0.0 copy-start.1
  23.3 16.8 %all-to-all-done.blocks = bf16[8,576,128]{2,1,0:T(8,128)(2,1)S(1)} async-done(((bf16[8,576,128]{2,1,0:T(8,128)(2,1)}), bf16[8,576,128]{2,1,0:T(8,128)(2,1)S(1)}, u32[]{:S(2)}, u32[]{:S(2)}) %all-to-all-start) | async-done | bytes 1179680 | tf_op jit(solution)/shard_map/all_to_all | solution.py:29
  40.1 0.9 sum_kernel.1
  41.0 0.0 copy-done.2
  41.0 12.1 %all-to-all-start.1 = ((bf16[48,12,128]{2,1,0:T(8,128)(2,1)}), bf16[48,12,128]{2,1,0:T(8,128)(2,1)S(1)}, u32[]{:S(2)}, u32[]{:S(2)}) async-start(bf16[48,12,128]{2,1,0:T(8,128)(2,1)} %sum_kernel.1), calls=%async_computation.1 | async-start | bytes 393216 | tf_op jit(solution)/shard_map/all_to_all | solution.py:29
  53.1 0.0 copy-done
  53.1 0.0 copy-done.1
  53.1 3.7 %collective-permute-start.1 = (f32[3,6,128]{2,1,0:T(8,128)S(1)}, f32[3,6,128]{2,1,0:T(8,128)S(1)}, u32[]{:S(2)}, u32[]{:S(2)}) collective-permute-start(f32[3,6,128]{2,1,0:T(8,128)S(1)} %select_bitcast_fusion), channel_id=1, source_target_pairs={{0,1},{1,0},{2,3},{3,2},{4,5},{5,4},{6,7},{7,6},{8,9},{9,8},{10,11... | collective-permute-start | bytes 27656 | tf_op jit(solution)/shard_map/ppermute | solution.py:230
  56.9 0.8 collective-permute-done.1
  57.7 10.7 %all-to-all-done.1.blocks = bf16[48,12,128]{2,1,0:T(8,128)(2,1)S(1)} async-done(((bf16[48,12,128]{2,1,0:T(8,128)(2,1)}), bf16[48,12,128]{2,1,0:T(8,128)(2,1)S(1)}, u32[]{:S(2)}, u32[]{:S(2)}) %all-to-all-start.1) | async-done | bytes 147488 | tf_op jit(solution)/shard_map/all_to_all | solution.py:29
  68.4 0.8 finish_kernel.1
  69.2 5.7 %all-to-all-start.2 = ((bf16[48,12,128]{2,1,0:T(8,128)(2,1)}), bf16[48,12,128]{2,1,0:T(8,128)(2,1)S(1)}, u32[]{:S(2)}, u32[]{:S(2)}) async-start(bf16[48,12,128]{2,1,0:T(8,128)(2,1)} %get-tuple-element.25), calls=%async_computation.2 | async-start | bytes 393216 | tf_op jit(solution)/shard_map/all_to_all | solution.py:29
  74.9 4.5 %collective-permute-start.2 = (f32[6,128]{1,0:T(8,128)S(1)}, f32[6,128]{1,0:T(8,128)S(1)}, u32[]{:S(2)}, u32[]{:S(2)}) collective-permute-start(f32[6,128]{1,0:T(8,128)S(1)} %slice_select_fusion.1), channel_id=1, source_target_pairs={{0,1},{1,0},{2,3},{3,2},{4,5},{5,4},{6,7},{7,6},{8,9},{9,8},{10,11... | collective-permute-start | bytes 9224 | tf_op jit(solution)/shard_map/ppermute | solution.py:237
  79.5 10.7 %all-to-all-done.2.blocks = bf16[48,12,128]{2,1,0:T(8,128)(2,1)S(1)} async-done(((bf16[48,12,128]{2,1,0:T(8,128)(2,1)}), bf16[48,12,128]{2,1,0:T(8,128)(2,1)S(1)}, u32[]{:S(2)}, u32[]{:S(2)}) %all-to-all-start.2) | async-done | bytes 147488 | tf_op jit(solution)/shard_map/all_to_all | solution.py:29
  90.2 0.1 spread_kernel.1
  90.3 0.0 collective-permute-done.2
  90.3 17.0 %all_to_all.20 = bf16[8,576,128]{2,1,0:T(8,128)(2,1)S(1)} all-to-all(bf16[8,576,128]{2,1,0:T(8,128)(2,1)S(1)} %spread_kernel.1), channel_id=1, replica_groups=mesh['yh'=2,'x'=4,'yl'=2,'yp'=2,'z'=12,'core'=2] {'x','yp'}, dimensions={0} | all-to-all | bytes 2359296 | tf_op jit(solution)/shard_map/all_to_all | solution.py:29
  107.3 7.4 %collective-permute-start.3 = (bf16[8,576,128]{2,1,0:T(8,128)(2,1)S(1)}, bf16[8,576,128]{2,1,0:T(8,128)(2,1)S(1)}, u32[]{:S(2)}, u32[]{:S(2)}) collective-permute-start(bf16[8,576,128]{2,1,0:T(8,128)(2,1)S(1)} %all_to_all.20), channel_id=1, source_target_pairs={{0,1},{1,0},{2,3},{3,2},{4,5},{5,4},{6,7},{7,6},{8,9},{9,8},{10,11... | collective-permute-start | bytes 3538952 | tf_op jit(solution)/shard_map/ppermute | solution.py:242
  114.7 1.1 write_kernel.2.refs_1_
  115.8 0.6 copy.17
  116.4 0.6 copy.18
  117.0 0.6 copy.19
  117.6 0.0 collective-permute-done.3
  117.6 1.1 write_kernel.3
  (9 shorter events, 0.1 us)
Async XLA Ops:
  3.5 14.9 %collective-permute-start = (bf16[8,576,128]{2,1,0:T(8,128)(2,1)S(1)}, bf16[8,576,128]{2,1,0:T(8,128)(2,1)S(1)}, u32[]{:S(2)}, u32[]{:S(2)}) collective-permute-start(bf16[8,576,128]{2,1,0:T(8,128)(2,1)S(1)} %get-tuple-element.19), channel_id=1, source_target_pairs={{0,1},{1,0},{2,3},{3,2},{4,5},{5,4},{6,7},{7,6},{8,9},{9,8},{10,11... | collective-permute-start | bytes 3538952 | tf_op jit(solution)/shard_map/ppermute | solution.py:224
  19.7 20.4 %all-to-all-start = ((bf16[8,576,128]{2,1,0:T(8,128)(2,1)}), bf16[8,576,128]{2,1,0:T(8,128)(2,1)S(1)}, u32[]{:S(2)}, u32[]{:S(2)}) async-start(bf16[8,576,128]{2,1,0:T(8,128)(2,1)} %add_kernel.1), calls=%async_computation | async-start | bytes 2359296 | tf_op jit(solution)/shard_map/all_to_all | solution.py:29
  23.2 17.8 %copy-start.2 = (f32[2,6,128]{2,0,1:T(2,128)S(1)}, f32[2,6,128]{2,0,1:T(2,128)}, u32[]{:S(2)}) copy-start(f32[2,6,128]{2,0,1:T(2,128)} %param.8) | copy-start | bytes 18436
  23.2 29.8 %copy-start = (f32[2,6,128]{2,0,1:T(2,128)S(1)}, f32[2,6,128]{2,0,1:T(2,128)}, u32[]{:S(2)}) copy-start(f32[2,6,128]{2,0,1:T(2,128)} %param.7) | copy-start | bytes 18436
  23.3 29.8 %copy-start.1 = (f32[2,6,128]{2,0,1:T(2,128)S(1)}, f32[2,6,128]{2,0,1:T(2,128)}, u32[]{:S(2)}) copy-start(f32[2,6,128]{2,0,1:T(2,128)} %param.9) | copy-start | bytes 18436
  41.0 27.4 %all-to-all-start.1 = ((bf16[48,12,128]{2,1,0:T(8,128)(2,1)}), bf16[48,12,128]{2,1,0:T(8,128)(2,1)S(1)}, u32[]{:S(2)}, u32[]{:S(2)}) async-start(bf16[48,12,128]{2,1,0:T(8,128)(2,1)} %sum_kernel.1), calls=%async_computation.1 | async-start | bytes 393216 | tf_op jit(solution)/shard_map/all_to_all | solution.py:29
  53.1 4.5 %collective-permute-start.1 = (f32[3,6,128]{2,1,0:T(8,128)S(1)}, f32[3,6,128]{2,1,0:T(8,128)S(1)}, u32[]{:S(2)}, u32[]{:S(2)}) collective-permute-start(f32[3,6,128]{2,1,0:T(8,128)S(1)} %select_bitcast_fusion), channel_id=1, source_target_pairs={{0,1},{1,0},{2,3},{3,2},{4,5},{5,4},{6,7},{7,6},{8,9},{9,8},{10,11... | collective-permute-start | bytes 27656 | tf_op jit(solution)/shard_map/ppermute | solution.py:230
  69.2 21.0 %all-to-all-start.2 = ((bf16[48,12,128]{2,1,0:T(8,128)(2,1)}), bf16[48,12,128]{2,1,0:T(8,128)(2,1)S(1)}, u32[]{:S(2)}, u32[]{:S(2)}) async-start(bf16[48,12,128]{2,1,0:T(8,128)(2,1)} %get-tuple-element.25), calls=%async_computation.2 | async-start | bytes 393216 | tf_op jit(solution)/shard_map/all_to_all | solution.py:29
  74.9 15.4 %collective-permute-start.2 = (f32[6,128]{1,0:T(8,128)S(1)}, f32[6,128]{1,0:T(8,128)S(1)}, u32[]{:S(2)}, u32[]{:S(2)}) collective-permute-start(f32[6,128]{1,0:T(8,128)S(1)} %slice_select_fusion.1), channel_id=1, source_target_pairs={{0,1},{1,0},{2,3},{3,2},{4,5},{5,4},{6,7},{7,6},{8,9},{9,8},{10,11... | collective-permute-start | bytes 9224 | tf_op jit(solution)/shard_map/ppermute | solution.py:237
  107.3 10.3 %collective-permute-start.3 = (bf16[8,576,128]{2,1,0:T(8,128)(2,1)S(1)}, bf16[8,576,128]{2,1,0:T(8,128)(2,1)S(1)}, u32[]{:S(2)}, u32[]{:S(2)}) collective-permute-start(bf16[8,576,128]{2,1,0:T(8,128)(2,1)S(1)} %all_to_all.20), channel_id=1, source_target_pairs={{0,1},{1,0},{2,3},{3,2},{4,5},{5,4},{6,7},{7,6},{8,9},{9,8},{10,11... | collective-permute-start | bytes 3538952 | tf_op jit(solution)/shard_map/ppermute | solution.py:242

commit v6 on v5

--- a/solution.py
+++ b/solution.py
@@ -222,12 +222,16 @@
 
     away, tokens, cotangents = first_gradient(tokens, cotangents)
     away = lax.ppermute(away, "core", SWAP)
-    near = sum_near(exchange(add(second_gradient(tokens, cotangents), away), NEAR))
-
-    params, moment, second, near = lax.optimization_barrier((params, moment, second, near))
+    home = second_gradient(tokens, cotangents)
+    params, moment, second, home = lax.optimization_barrier((params, moment, second, home))
     state = jnp.stack([params, moment, second], axis=1)
     home_state = jnp.where(first, state[0], state[1])
-    other_state = lax.ppermute(jnp.where(first, state[1], state[0]), "core", SWAP)
+    other_state = jnp.where(first, state[1], state[0])
+    home_state, other_state, away = lax.optimization_barrier((home_state, other_state, away))
+    near = sum_near(exchange(add(home, away), NEAR))
+
+    other_state, near = lax.optimization_barrier((other_state, near))
+    other_state = lax.ppermute(other_state, "core", SWAP)
     held = in_order(first, home_state, other_state, 1)
 
     gradient, rounded = finish(exchange(near, FAR), held)

time: 119 us -> 117 us (0.983)
  waiting for transfers between devices: 40.5 us -> 20.9 us
  blocking collectives: 17 us -> 35.8 us
  starting transfers between devices: 49.4 us -> 47.4 us
    all_to_all x1 -> x2, blocking collectives: 17 us -> 35.8 us  [exchange(): return lax.all_to_all(blocks, axes, 0, 0, tiled=True)]
    all_to_all x3 -> x2, waiting for transfers between devices: 38.2 us -> 20 us  [exchange(): return lax.all_to_all(blocks, axes, 0, 0, tiled=True)]
    all_to_all x3 -> x2, starting transfers between devices: 21.4 us -> 17.6 us  [exchange(): return lax.all_to_all(blocks, axes, 0, 0, tiled=True)]
    ppermute x1, waiting for transfers between devices: 1.48 us -> 0.11 us  [on_device(): away = lax.ppermute(away, 'core', SWAP)]
    ppermute x1, starting transfers between devices: 4.55 us -> 5.78 us  [on_device(): lax.ppermute(jnp.where(first, gradient[6:], gradient[:6]), 'core', SWAP)]
  transfers between devices with their start and end apart: 7 -> 6, of which waited for: 5 -> 4; matrix products, arithmetic and copies ran while one was open for 2% -> 3% of each run, Pallas kernels for 2% -> 2%
where the time goes in v6:
time: 117 us; the launch traced here: 116 us
  starting transfers between devices  47.4 us (41%)
  blocking collectives  35.8 us (31%)
  waiting for transfers between devices  20.9 us (18%)
  Pallas kernels  8.03 us (7%)
  local copies, waits for them, and re-layouts  2.53 us (2%)
    all_to_all x2, blocking collectives, exchange(): return lax.all_to_all(blocks, axes, 0, 0, tiled=True)  35.8 us
    all_to_all x2, waiting for transfers between devices, exchange(): return lax.all_to_all(blocks, axes, 0, 0, tiled=True)  20 us
    all_to_all x2, starting transfers between devices, exchange(): return lax.all_to_all(blocks, axes, 0, 0, tiled=True)  17.6 us
    ppermute x1, starting transfers between devices, on_device(): away = lax.ppermute(away, 'core', SWAP)  12.4 us
    ppermute x1, starting transfers between devices, on_device(): theirs = lax.ppermute(mine, 'core', SWAP)  7.52 us
    ppermute x1, starting transfers between devices, on_device(): lax.ppermute(jnp.where(first, gradient[6:], gradient[:6]), 'core', SWAP)  5.78 us
    ppermute x1, starting transfers between devices, on_device(): other_state = lax.ppermute(other_state, 'core', SWAP)  4.09 us
    pallas_call x1, Pallas kernels, first_gradient(): pl.pallas_call(first_kernel, out_shape=[NEAR_BLOCKS, pltpu.VMEM(tokens.sh...  2.85 us
  transfers between devices with their start and end apart: 6, of which 4 were waited for; matrix products, arithmetic and copies ran while one was open for 3% of the time, Pallas kernels for 2%

profile of v6, /device:TPU:1, one launch (start us, length us, event | category | flops | bytes accessed | tf_op | source)
XLA Modules:
  0.0 116.2 jit_solution(17807537093902409817)
XLA Ops:
  0.6 2.8 %first_kernel.1 = (bf16[8,576,128]{2,1,0:T(8,128)(2,1)S(1)}, bf16[384,4608]{1,0:T(8,128)(2,1)S(1)}, bf16[2,384,128]{2,1,0:T(8,128)(2,1)S(1)}) custom-call(bf16[384,4608]{1,0:T(8,128)(2,1)} %tokens.1, bf16[2,384,128]{2,1,0:T(8,128)(2,1)} %cotangents.1), custom_call_target="tpu_custom_call" | custom-call | tf_op jit(solution)/shard_map/first_kernel/pallas_call | solution.py:70
  3.5 12.4 %collective-permute-start = (bf16[8,576,128]{2,1,0:T(8,128)(2,1)S(1)}, bf16[8,576,128]{2,1,0:T(8,128)(2,1)S(1)}, u32[]{:S(2)}, u32[]{:S(2)}) collective-permute-start(bf16[8,576,128]{2,1,0:T(8,128)(2,1)S(1)} %get-tuple-element.27), channel_id=1, source_target_pairs={{0,1},{1,0},{2,3},{3,2},{4,5},{5,4},{6,7},{7,6},{8,9},{9,8},{10,11... | collective-permute-start | bytes 3538952 | tf_op jit(solution)/shard_map/ppermute | solution.py:224
  15.9 0.0 copy-start.3
  15.9 0.0 copy-start
  16.0 1.0 second_kernel.1.left
  16.9 0.0 copy-done.3
  16.9 0.0 copy-done
  17.0 0.7 copy_bitcast_fusion
  17.7 0.6 select_bitcast_fusion
  18.3 0.1 collective-permute-done.right
  18.4 0.3 add_kernel.1
  18.6 19.3 %all_to_all.20.blocks = bf16[8,576,128]{2,1,0:T(8,128)(2,1)S(1)} all-to-all(bf16[8,576,128]{2,1,0:T(8,128)(2,1)S(1)} %add_kernel.1), channel_id=1, replica_groups=mesh['yh'=2,'x'=4,'yl'=2,'yp'=2,'z'=12,'core'=2] {'x','yp'}, dimensions={0} | all-to-all | bytes 2359296 | tf_op jit(solution)/shard_map/all_to_all | solution.py:29
  37.9 0.0 copy-start.5
  37.9 0.9 sum_kernel.1
  38.8 12.7 %all-to-all-start.1 = ((bf16[48,12,128]{2,1,0:T(8,128)(2,1)}), bf16[48,12,128]{2,1,0:T(8,128)(2,1)S(1)}, u32[]{:S(2)}, u32[]{:S(2)}) async-start(bf16[48,12,128]{2,1,0:T(8,128)(2,1)} %sum_kernel.1), calls=%async_computation.1 | async-start | bytes 393216 | tf_op jit(solution)/shard_map/all_to_all | solution.py:29
  51.6 0.0 copy-done.5
  51.6 4.1 %collective-permute-start.1 = (f32[3,6,128]{2,1,0:T(8,128)S(1)}, f32[3,6,128]{2,1,0:T(8,128)S(1)}, u32[]{:S(2)}, u32[]{:S(2)}) collective-permute-start(f32[3,6,128]{2,1,0:T(8,128)S(1)} %copy-done.5), channel_id=1, source_target_pairs={{0,1},{1,0},{2,3},{3,2},{4,5},{5,4},{6,7},{7,6},{8,9},{9,8},{10,11... | collective-permute-start | bytes 27656 | tf_op jit(solution)/shard_map/ppermute | solution.py:234
  55.7 0.8 collective-permute-done.1
  56.5 10.4 %all-to-all-done.1.blocks = bf16[48,12,128]{2,1,0:T(8,128)(2,1)S(1)} async-done(((bf16[48,12,128]{2,1,0:T(8,128)(2,1)}), bf16[48,12,128]{2,1,0:T(8,128)(2,1)S(1)}, u32[]{:S(2)}, u32[]{:S(2)}) %all-to-all-start.1) | async-done | bytes 147488 | tf_op jit(solution)/shard_map/all_to_all | solution.py:29
  66.9 0.8 finish_kernel.1
  67.7 4.9 %all-to-all-start.2 = ((bf16[48,12,128]{2,1,0:T(8,128)(2,1)}), bf16[48,12,128]{2,1,0:T(8,128)(2,1)S(1)}, u32[]{:S(2)}, u32[]{:S(2)}) async-start(bf16[48,12,128]{2,1,0:T(8,128)(2,1)} %get-tuple-element.35), calls=%async_computation.2 | async-start | bytes 393216 | tf_op jit(solution)/shard_map/all_to_all | solution.py:29
  72.6 5.8 %collective-permute-start.2 = (f32[6,128]{1,0:T(8,128)S(1)}, f32[6,128]{1,0:T(8,128)S(1)}, u32[]{:S(2)}, u32[]{:S(2)}) collective-permute-start(f32[6,128]{1,0:T(8,128)S(1)} %slice_select_fusion), channel_id=1, source_target_pairs={{0,1},{1,0},{2,3},{3,2},{4,5},{5,4},{6,7},{7,6},{8,9},{9,8},{10,11... | collective-permute-start | bytes 9224 | tf_op jit(solution)/shard_map/ppermute | solution.py:241
  78.4 9.6 %all-to-all-done.2.blocks = bf16[48,12,128]{2,1,0:T(8,128)(2,1)S(1)} async-done(((bf16[48,12,128]{2,1,0:T(8,128)(2,1)}), bf16[48,12,128]{2,1,0:T(8,128)(2,1)S(1)}, u32[]{:S(2)}, u32[]{:S(2)}) %all-to-all-start.2) | async-done | bytes 147488 | tf_op jit(solution)/shard_map/all_to_all | solution.py:29
  88.0 0.1 spread_kernel.1
  88.1 0.0 collective-permute-done.2
  88.1 16.5 %all_to_all.21 = bf16[8,576,128]{2,1,0:T(8,128)(2,1)S(1)} all-to-all(bf16[8,576,128]{2,1,0:T(8,128)(2,1)S(1)} %spread_kernel.1), channel_id=1, replica_groups=mesh['yh'=2,'x'=4,'yl'=2,'yp'=2,'z'=12,'core'=2] {'x','yp'}, dimensions={0} | all-to-all | bytes 2359296 | tf_op jit(solution)/shard_map/all_to_all | solution.py:29
  104.6 7.5 %collective-permute-start.3 = (bf16[8,576,128]{2,1,0:T(8,128)(2,1)S(1)}, bf16[8,576,128]{2,1,0:T(8,128)(2,1)S(1)}, u32[]{:S(2)}, u32[]{:S(2)}) collective-permute-start(bf16[8,576,128]{2,1,0:T(8,128)(2,1)S(1)} %all_to_all.21), channel_id=1, source_target_pairs={{0,1},{1,0},{2,3},{3,2},{4,5},{5,4},{6,7},{7,6},{8,9},{9,8},{10,11... | collective-permute-start | bytes 3538952 | tf_op jit(solution)/shard_map/ppermute | solution.py:246
  112.1 0.0 copy-start.1
  112.1 0.0 copy-start.2
  112.1 0.0 copy-start.4
  112.1 1.1 write_kernel.2.refs_1_
  113.2 0.0 copy-done.1
  113.2 0.0 copy-done.2
  113.3 0.0 copy-done.4
  113.3 0.6 copy.17
  113.9 0.6 copy.18
  114.5 0.6 copy.19
  115.1 0.0 collective-permute-done.3
  115.1 1.1 write_kernel.3
  (7 shorter events, 0.1 us)
Async XLA Ops:
  3.5 14.9 %collective-permute-start = (bf16[8,576,128]{2,1,0:T(8,128)(2,1)S(1)}, bf16[8,576,128]{2,1,0:T(8,128)(2,1)S(1)}, u32[]{:S(2)}, u32[]{:S(2)}) collective-permute-start(bf16[8,576,128]{2,1,0:T(8,128)(2,1)S(1)} %get-tuple-element.27), channel_id=1, source_target_pairs={{0,1},{1,0},{2,3},{3,2},{4,5},{5,4},{6,7},{7,6},{8,9},{9,8},{10,11... | collective-permute-start | bytes 3538952 | tf_op jit(solution)/shard_map/ppermute | solution.py:224
  15.9 1.0 copy-start.3
  15.9 1.0 copy-start
  37.9 13.6 %copy-start.5 = (f32[3,6,128]{2,1,0:T(8,128)S(1)}, f32[3,6,128]{2,1,0:T(8,128)}, u32[]{:S(2)}) copy-start(f32[3,6,128]{2,1,0:T(8,128)} %get-tuple-element.33) | copy-start | bytes 27652
  38.8 28.1 %all-to-all-start.1 = ((bf16[48,12,128]{2,1,0:T(8,128)(2,1)}), bf16[48,12,128]{2,1,0:T(8,128)(2,1)S(1)}, u32[]{:S(2)}, u32[]{:S(2)}) async-start(bf16[48,12,128]{2,1,0:T(8,128)(2,1)} %sum_kernel.1), calls=%async_computation.1 | async-start | bytes 393216 | tf_op jit(solution)/shard_map/all_to_all | solution.py:29
  51.6 4.9 %collective-permute-start.1 = (f32[3,6,128]{2,1,0:T(8,128)S(1)}, f32[3,6,128]{2,1,0:T(8,128)S(1)}, u32[]{:S(2)}, u32[]{:S(2)}) collective-permute-start(f32[3,6,128]{2,1,0:T(8,128)S(1)} %copy-done.5), channel_id=1, source_target_pairs={{0,1},{1,0},{2,3},{3,2},{4,5},{5,4},{6,7},{7,6},{8,9},{9,8},{10,11... | collective-permute-start | bytes 27656 | tf_op jit(solution)/shard_map/ppermute | solution.py:234
  67.7 20.3 %all-to-all-start.2 = ((bf16[48,12,128]{2,1,0:T(8,128)(2,1)}), bf16[48,12,128]{2,1,0:T(8,128)(2,1)S(1)}, u32[]{:S(2)}, u32[]{:S(2)}) async-start(bf16[48,12,128]{2,1,0:T(8,128)(2,1)} %get-tuple-element.35), calls=%async_computation.2 | async-start | bytes 393216 | tf_op jit(solution)/shard_map/all_to_all | solution.py:29
  72.6 15.5 %collective-permute-start.2 = (f32[6,128]{1,0:T(8,128)S(1)}, f32[6,128]{1,0:T(8,128)S(1)}, u32[]{:S(2)}, u32[]{:S(2)}) collective-permute-start(f32[6,128]{1,0:T(8,128)S(1)} %slice_select_fusion), channel_id=1, source_target_pairs={{0,1},{1,0},{2,3},{3,2},{4,5},{5,4},{6,7},{7,6},{8,9},{9,8},{10,11... | collective-permute-start | bytes 9224 | tf_op jit(solution)/shard_map/ppermute | solution.py:241
  104.6 10.5 %collective-permute-start.3 = (bf16[8,576,128]{2,1,0:T(8,128)(2,1)S(1)}, bf16[8,576,128]{2,1,0:T(8,128)(2,1)S(1)}, u32[]{:S(2)}, u32[]{:S(2)}) collective-permute-start(bf16[8,576,128]{2,1,0:T(8,128)(2,1)S(1)} %all_to_all.21), channel_id=1, source_target_pairs={{0,1},{1,0},{2,3},{3,2},{4,5},{5,4},{6,7},{7,6},{8,9},{9,8},{10,11... | collective-permute-start | bytes 3538952 | tf_op jit(solution)/shard_map/ppermute | solution.py:246
  112.1 1.1 copy-start.1
  112.1 1.1 copy-start.2
  112.1 1.1 copy-start.4

commit v7 on v6

--- a/solution.py
+++ b/solution.py
@@ -11,13 +11,14 @@
 ALL = ("yh", "x", "yl", "yp", "z", "core")
 SIZES = (2, 4, 2, 2, 12, 2)
 NEAR = ("x", "yp")
-FAR = ("yh", "yl", "z")
+FAR = ("yl", "z", "yh")
 SWAP = [(0, 1), (1, 0)]
 N_NEAR, N_FAR = 8, 48
 D, COLS = 4608, 128
 ROWS = 12
 BLOCK = 144
 STEP = 1152
+FETCHES = ((0, 3), (3, 4))
 
 VMEM = pl.BlockSpec(memory_space=pltpu.VMEM)
 PARAMS = pltpu.CompilerParams(vmem_limit_bytes=24 * 2**20)
@@ -32,6 +33,12 @@
 def place(block):
     yh, x, yl, yp = block // 16, block // 4 % 4, block // 2 % 2, block % 2
     return x * 2 + yp, (yh * 2 + yl) * BLOCK
+
+
+def far_rows(index):
+    yl, z, yh = index // 24, index // 2 % 12, index % 2
+    first = ((yh * 2 + yl) * 12 + z) * ROWS
+    return slice(first, first + ROWS)
 
 
 def multiply(tokens, cotangent, out, columns):
@@ -49,17 +56,17 @@
 def first_kernel(tokens, cotangents, out, held, small, arrived):
     other = 1 - lax.axis_index("core")
     copies = [pltpu.make_async_copy(cotangents, small, arrived.at[2])]
-    for half in range(2):
-        columns = (slice(None), pl.ds(half * (D // 2), D // 2))
+    for index, (first, last) in enumerate(FETCHES):
+        columns = (slice(None), pl.ds(first * STEP, (last - first) * STEP))
         copies.append(
-            pltpu.make_async_copy(tokens.at[columns], held.at[columns], arrived.at[half])
+            pltpu.make_async_copy(tokens.at[columns], held.at[columns], arrived.at[index])
         )
     for copy in copies:
         copy.start()
     copies[0].wait()
-    for half in range(2):
-        copies[1 + half].wait()
-        multiply(held, small[other], out, (2 * half, 2 * half + 1))
+    for copy, (first, last) in zip(copies[1:], FETCHES):
+        copy.wait()
+        multiply(held, small[other], out, range(first, last))
 
 
 def second_kernel(tokens, cotangents, out):
@@ -116,7 +123,7 @@
 def sum_kernel(blocks, out, held):
     held[...] = blocks[...].astype(jnp.float32).sum(0)
     for index in range(N_FAR):
-        out[index] = held[index * ROWS : (index + 1) * ROWS, :].astype(out.dtype)
+        out[index] = held[far_rows(index), :].astype(out.dtype)
 
 
 def sum_near(blocks):
@@ -133,7 +140,7 @@
 
 def spread_kernel(blocks, out, held):
     for index in range(N_FAR):
-        held[index * ROWS : (index + 1) * ROWS, :] = blocks[index].astype(jnp.float32)
+        held[far_rows(index), :] = blocks[index].astype(jnp.float32)
     rows = held[...].astype(out.dtype)
     for index in range(N_NEAR):
         out[index] = rows

time: 117 us -> 116 us (level)
  waiting for transfers between devices: 20.9 us -> 19.5 us
    all_to_all x2, starting transfers between devices: 17.6 us -> 19.4 us  [exchange(): return lax.all_to_all(blocks, axes, 0, 0, tiled=True)]
    all_to_all x2, waiting for transfers between devices: 20 us -> 18.6 us  [exchange(): return lax.all_to_all(blocks, axes, 0, 0, tiled=True)]
where the time goes in v7:
time: 116 us; the launch traced here: 115 us
  starting transfers between devices  47.5 us (41%)
  blocking collectives  36 us (31%)
  waiting for transfers between devices  19.5 us (17%)
  Pallas kernels  8.3 us (7%)
  local copies, waits for them, and re-layouts  2.53 us (2%)
    all_to_all x2, blocking collectives, exchange(): return lax.all_to_all(blocks, axes, 0, 0, tiled=True)  36 us
    all_to_all x2, starting transfers between devices, exchange(): return lax.all_to_all(blocks, axes, 0, 0, tiled=True)  19.4 us
    all_to_all x2, waiting for transfers between devices, exchange(): return lax.all_to_all(blocks, axes, 0, 0, tiled=True)  18.6 us
    ppermute x1, starting transfers between devices, on_device(): away = lax.ppermute(away, 'core', SWAP)  12.4 us
    ppermute x1, starting transfers between devices, on_device(): theirs = lax.ppermute(mine, 'core', SWAP)  6.91 us
    ppermute x1, starting transfers between devices, on_device(): lax.ppermute(jnp.where(first, gradient[6:], gradient[:6]), 'core', SWAP)  4.68 us
    ppermute x1, starting transfers between devices, on_device(): other_state = lax.ppermute(other_state, 'core', SWAP)  4.09 us
    pallas_call x1, Pallas kernels, first_gradient(): pl.pallas_call(first_kernel, out_shape=[NEAR_BLOCKS, pltpu.VMEM(tokens.sh...  3.12 us
  transfers between devices with their start and end apart: 6, of which 4 were waited for; matrix products, arithmetic and copies ran while one was open for 3% of the time, Pallas kernels for 2%

profile of v7, /device:TPU:1, one launch (start us, length us, event | category | flops | bytes accessed | tf_op | source)
XLA Modules:
  0.0 115.3 jit_solution(5255549857331179420)
XLA Ops:
  0.6 3.1 %first_kernel.1 = (bf16[8,576,128]{2,1,0:T(8,128)(2,1)S(1)}, bf16[384,4608]{1,0:T(8,128)(2,1)S(1)}, bf16[2,384,128]{2,1,0:T(8,128)(2,1)S(1)}) custom-call(bf16[384,4608]{1,0:T(8,128)(2,1)} %tokens.1, bf16[2,384,128]{2,1,0:T(8,128)(2,1)} %cotangents.1), custom_call_target="tpu_custom_call" | custom-call | tf_op jit(solution)/shard_map/first_kernel/pallas_call | solution.py:77
  3.8 12.4 %collective-permute-start = (bf16[8,576,128]{2,1,0:T(8,128)(2,1)S(1)}, bf16[8,576,128]{2,1,0:T(8,128)(2,1)S(1)}, u32[]{:S(2)}, u32[]{:S(2)}) collective-permute-start(bf16[8,576,128]{2,1,0:T(8,128)(2,1)S(1)} %get-tuple-element.27), channel_id=1, source_target_pairs={{0,1},{1,0},{2,3},{3,2},{4,5},{5,4},{6,7},{7,6},{8,9},{9,8},{10,11... | collective-permute-start | bytes 3538952 | tf_op jit(solution)/shard_map/ppermute | solution.py:231
  16.2 0.0 copy-start.3
  16.2 0.0 copy-start
  16.2 1.0 second_kernel.1.left
  17.2 0.0 copy-done.3
  17.2 0.0 copy-done
  17.2 0.7 copy_bitcast_fusion
  17.9 0.6 select_bitcast_fusion
  18.5 0.1 collective-permute-done.right
  18.6 0.3 add_kernel.1
  18.9 19.3 %all_to_all.20.blocks = bf16[8,576,128]{2,1,0:T(8,128)(2,1)S(1)} all-to-all(bf16[8,576,128]{2,1,0:T(8,128)(2,1)S(1)} %add_kernel.1), channel_id=1, replica_groups=mesh['yh'=2,'x'=4,'yl'=2,'yp'=2,'z'=12,'core'=2] {'x','yp'}, dimensions={0} | all-to-all | bytes 2359296 | tf_op jit(solution)/shard_map/all_to_all | solution.py:30
  38.2 0.0 copy-start.5
  38.2 0.9 sum_kernel.1
  39.1 12.7 %all-to-all-start.1 = ((bf16[48,12,128]{2,1,0:T(8,128)(2,1)}), bf16[48,12,128]{2,1,0:T(8,128)(2,1)S(1)}, u32[]{:S(2)}, u32[]{:S(2)}) async-start(bf16[48,12,128]{2,1,0:T(8,128)(2,1)} %sum_kernel.1), calls=%async_computation.1 | async-start | bytes 393216 | tf_op jit(solution)/shard_map/all_to_all | solution.py:30
  51.8 0.0 copy-done.5
  51.9 4.1 %collective-permute-start.1 = (f32[3,6,128]{2,1,0:T(8,128)S(1)}, f32[3,6,128]{2,1,0:T(8,128)S(1)}, u32[]{:S(2)}, u32[]{:S(2)}) collective-permute-start(f32[3,6,128]{2,1,0:T(8,128)S(1)} %copy-done.5), channel_id=1, source_target_pairs={{0,1},{1,0},{2,3},{3,2},{4,5},{5,4},{6,7},{7,6},{8,9},{9,8},{10,11... | collective-permute-start | bytes 27656 | tf_op jit(solution)/shard_map/ppermute | solution.py:241
  56.0 0.8 collective-permute-done.1
  56.8 9.2 %all-to-all-done.1.blocks = bf16[48,12,128]{2,1,0:T(8,128)(2,1)S(1)} async-done(((bf16[48,12,128]{2,1,0:T(8,128)(2,1)}), bf16[48,12,128]{2,1,0:T(8,128)(2,1)S(1)}, u32[]{:S(2)}, u32[]{:S(2)}) %all-to-all-start.1) | async-done | bytes 147488 | tf_op jit(solution)/shard_map/all_to_all | solution.py:30
  65.9 0.8 finish_kernel.1
  66.7 6.6 %all-to-all-start.2 = ((bf16[48,12,128]{2,1,0:T(8,128)(2,1)}), bf16[48,12,128]{2,1,0:T(8,128)(2,1)S(1)}, u32[]{:S(2)}, u32[]{:S(2)}) async-start(bf16[48,12,128]{2,1,0:T(8,128)(2,1)} %get-tuple-element.35), calls=%async_computation.2 | async-start | bytes 393216 | tf_op jit(solution)/shard_map/all_to_all | solution.py:30
  73.4 4.7 %collective-permute-start.2 = (f32[6,128]{1,0:T(8,128)S(1)}, f32[6,128]{1,0:T(8,128)S(1)}, u32[]{:S(2)}, u32[]{:S(2)}) collective-permute-start(f32[6,128]{1,0:T(8,128)S(1)} %slice_select_fusion), channel_id=1, source_target_pairs={{0,1},{1,0},{2,3},{3,2},{4,5},{5,4},{6,7},{7,6},{8,9},{9,8},{10,11... | collective-permute-start | bytes 9224 | tf_op jit(solution)/shard_map/ppermute | solution.py:248
  78.1 9.4 %all-to-all-done.2.blocks = bf16[48,12,128]{2,1,0:T(8,128)(2,1)S(1)} async-done(((bf16[48,12,128]{2,1,0:T(8,128)(2,1)}), bf16[48,12,128]{2,1,0:T(8,128)(2,1)S(1)}, u32[]{:S(2)}, u32[]{:S(2)}) %all-to-all-start.2) | async-done | bytes 147488 | tf_op jit(solution)/shard_map/all_to_all | solution.py:30
  87.5 0.1 spread_kernel.1
  87.6 0.0 collective-permute-done.2
  87.6 16.7 %all_to_all.21 = bf16[8,576,128]{2,1,0:T(8,128)(2,1)S(1)} all-to-all(bf16[8,576,128]{2,1,0:T(8,128)(2,1)S(1)} %spread_kernel.1), channel_id=1, replica_groups=mesh['yh'=2,'x'=4,'yl'=2,'yp'=2,'z'=12,'core'=2] {'x','yp'}, dimensions={0} | all-to-all | bytes 2359296 | tf_op jit(solution)/shard_map/all_to_all | solution.py:30
  104.3 6.9 %collective-permute-start.3 = (bf16[8,576,128]{2,1,0:T(8,128)(2,1)S(1)}, bf16[8,576,128]{2,1,0:T(8,128)(2,1)S(1)}, u32[]{:S(2)}, u32[]{:S(2)}) collective-permute-start(bf16[8,576,128]{2,1,0:T(8,128)(2,1)S(1)} %all_to_all.21), channel_id=1, source_target_pairs={{0,1},{1,0},{2,3},{3,2},{4,5},{5,4},{6,7},{7,6},{8,9},{9,8},{10,11... | collective-permute-start | bytes 3538952 | tf_op jit(solution)/shard_map/ppermute | solution.py:253
  111.2 0.0 copy-start.1
  111.2 0.0 copy-start.2
  111.3 0.0 copy-start.4
  111.3 1.1 write_kernel.2.refs_1_
  112.4 0.0 copy-done.1
  112.4 0.0 copy-done.2
  112.4 0.0 copy-done.4
  112.4 0.6 copy.17
  113.0 0.6 copy.18
  113.6 0.6 copy.19
  114.2 0.0 collective-permute-done.3
  114.2 1.1 write_kernel.3
  (7 shorter events, 0.1 us)
Async XLA Ops:
  3.8 14.9 %collective-permute-start = (bf16[8,576,128]{2,1,0:T(8,128)(2,1)S(1)}, bf16[8,576,128]{2,1,0:T(8,128)(2,1)S(1)}, u32[]{:S(2)}, u32[]{:S(2)}) collective-permute-start(bf16[8,576,128]{2,1,0:T(8,128)(2,1)S(1)} %get-tuple-element.27), channel_id=1, source_target_pairs={{0,1},{1,0},{2,3},{3,2},{4,5},{5,4},{6,7},{7,6},{8,9},{9,8},{10,11... | collective-permute-start | bytes 3538952 | tf_op jit(solution)/shard_map/ppermute | solution.py:231
  16.2 1.0 copy-start.3
  16.2 1.0 copy-start
  38.2 13.7 %copy-start.5 = (f32[3,6,128]{2,1,0:T(8,128)S(1)}, f32[3,6,128]{2,1,0:T(8,128)}, u32[]{:S(2)}) copy-start(f32[3,6,128]{2,1,0:T(8,128)} %get-tuple-element.33) | copy-start | bytes 27652
  39.1 26.8 %all-to-all-start.1 = ((bf16[48,12,128]{2,1,0:T(8,128)(2,1)}), bf16[48,12,128]{2,1,0:T(8,128)(2,1)S(1)}, u32[]{:S(2)}, u32[]{:S(2)}) async-start(bf16[48,12,128]{2,1,0:T(8,128)(2,1)} %sum_kernel.1), calls=%async_computation.1 | async-start | bytes 393216 | tf_op jit(solution)/shard_map/all_to_all | solution.py:30
  51.9 4.9 %collective-permute-start.1 = (f32[3,6,128]{2,1,0:T(8,128)S(1)}, f32[3,6,128]{2,1,0:T(8,128)S(1)}, u32[]{:S(2)}, u32[]{:S(2)}) collective-permute-start(f32[3,6,128]{2,1,0:T(8,128)S(1)} %copy-done.5), channel_id=1, source_target_pairs={{0,1},{1,0},{2,3},{3,2},{4,5},{5,4},{6,7},{7,6},{8,9},{9,8},{10,11... | collective-permute-start | bytes 27656 | tf_op jit(solution)/shard_map/ppermute | solution.py:241
  66.7 20.7 %all-to-all-start.2 = ((bf16[48,12,128]{2,1,0:T(8,128)(2,1)}), bf16[48,12,128]{2,1,0:T(8,128)(2,1)S(1)}, u32[]{:S(2)}, u32[]{:S(2)}) async-start(bf16[48,12,128]{2,1,0:T(8,128)(2,1)} %get-tuple-element.35), calls=%async_computation.2 | async-start | bytes 393216 | tf_op jit(solution)/shard_map/all_to_all | solution.py:30
  73.4 14.2 %collective-permute-start.2 = (f32[6,128]{1,0:T(8,128)S(1)}, f32[6,128]{1,0:T(8,128)S(1)}, u32[]{:S(2)}, u32[]{:S(2)}) collective-permute-start(f32[6,128]{1,0:T(8,128)S(1)} %slice_select_fusion), channel_id=1, source_target_pairs={{0,1},{1,0},{2,3},{3,2},{4,5},{5,4},{6,7},{7,6},{8,9},{9,8},{10,11... | collective-permute-start | bytes 9224 | tf_op jit(solution)/shard_map/ppermute | solution.py:248
  104.3 9.9 %collective-permute-start.3 = (bf16[8,576,128]{2,1,0:T(8,128)(2,1)S(1)}, bf16[8,576,128]{2,1,0:T(8,128)(2,1)S(1)}, u32[]{:S(2)}, u32[]{:S(2)}) collective-permute-start(bf16[8,576,128]{2,1,0:T(8,128)(2,1)S(1)} %all_to_all.21), channel_id=1, source_target_pairs={{0,1},{1,0},{2,3},{3,2},{4,5},{5,4},{6,7},{7,6},{8,9},{9,8},{10,11... | collective-permute-start | bytes 3538952 | tf_op jit(solution)/shard_map/ppermute | solution.py:253
  111.2 1.1 copy-start.1
  111.2 1.1 copy-start.2
  111.3 1.1 copy-start.4

commit v8 on v7

--- a/solution.py
+++ b/solution.py
@@ -18,7 +18,7 @@
 ROWS = 12
 BLOCK = 144
 STEP = 1152
-FETCHES = ((0, 3), (3, 4))
+FETCHES = ((0, 2), (2, 4))
 
 VMEM = pl.BlockSpec(memory_space=pltpu.VMEM)
 PARAMS = pltpu.CompilerParams(vmem_limit_bytes=24 * 2**20)

time: 116 us -> 115 us (level)
  no operation moved by 1% of the time
where the time goes in v8:
time: 115 us
  starting transfers between devices  47.5 us (41%)
  blocking collectives  36 us (31%)
  waiting for transfers between devices  19.5 us (17%)
  Pallas kernels  8.03 us (7%)
  local copies, waits for them, and re-layouts  2.53 us (2%)
    all_to_all x2, blocking collectives, exchange(): return lax.all_to_all(blocks, axes, 0, 0, tiled=True)  36 us
    all_to_all x2, starting transfers between devices, exchange(): return lax.all_to_all(blocks, axes, 0, 0, tiled=True)  19.4 us
    all_to_all x2, waiting for transfers between devices, exchange(): return lax.all_to_all(blocks, axes, 0, 0, tiled=True)  18.6 us
    ppermute x1, starting transfers between devices, on_device(): away = lax.ppermute(away, 'core', SWAP)  12.4 us
    ppermute x1, starting transfers between devices, on_device(): theirs = lax.ppermute(mine, 'core', SWAP)  6.91 us
    ppermute x1, starting transfers between devices, on_device(): lax.ppermute(jnp.where(first, gradient[6:], gradient[:6]), 'core', SWAP)  4.68 us
    ppermute x1, starting transfers between devices, on_device(): other_state = lax.ppermute(other_state, 'core', SWAP)  4.09 us
    pallas_call x1, Pallas kernels, first_gradient(): pl.pallas_call(first_kernel, out_shape=[NEAR_BLOCKS, pltpu.VMEM(tokens.sh...  2.85 us
  transfers between devices with their start and end apart: 6, of which 4 were waited for; matrix products, arithmetic and copies ran while one was open for 3% of the time, Pallas kernels for 2%

profile of v8, /device:TPU:1, one launch (start us, length us, event | category | flops | bytes accessed | tf_op | source)
XLA Modules:
  0.0 115.0 jit_solution(5023261217179879499)
XLA Ops:
  0.6 2.8 %first_kernel.1 = (bf16[8,576,128]{2,1,0:T(8,128)(2,1)S(1)}, bf16[384,4608]{1,0:T(8,128)(2,1)S(1)}, bf16[2,384,128]{2,1,0:T(8,128)(2,1)S(1)}) custom-call(bf16[384,4608]{1,0:T(8,128)(2,1)} %tokens.1, bf16[2,384,128]{2,1,0:T(8,128)(2,1)} %cotangents.1), custom_call_target="tpu_custom_call" | custom-call | tf_op jit(solution)/shard_map/first_kernel/pallas_call | solution.py:77
  3.5 12.4 %collective-permute-start = (bf16[8,576,128]{2,1,0:T(8,128)(2,1)S(1)}, bf16[8,576,128]{2,1,0:T(8,128)(2,1)S(1)}, u32[]{:S(2)}, u32[]{:S(2)}) collective-permute-start(bf16[8,576,128]{2,1,0:T(8,128)(2,1)S(1)} %get-tuple-element.27), channel_id=1, source_target_pairs={{0,1},{1,0},{2,3},{3,2},{4,5},{5,4},{6,7},{7,6},{8,9},{9,8},{10,11... | collective-permute-start | bytes 3538952 | tf_op jit(solution)/shard_map/ppermute | solution.py:231
  15.9 0.0 copy-start.3
  15.9 0.0 copy-start
  16.0 1.0 second_kernel.1.left
  16.9 0.0 copy-done.3
  16.9 0.0 copy-done
  17.0 0.7 copy_bitcast_fusion
  17.7 0.6 select_bitcast_fusion
  18.3 0.1 collective-permute-done.right
  18.4 0.3 add_kernel.1
  18.6 19.3 %all_to_all.20.blocks = bf16[8,576,128]{2,1,0:T(8,128)(2,1)S(1)} all-to-all(bf16[8,576,128]{2,1,0:T(8,128)(2,1)S(1)} %add_kernel.1), channel_id=1, replica_groups=mesh['yh'=2,'x'=4,'yl'=2,'yp'=2,'z'=12,'core'=2] {'x','yp'}, dimensions={0} | all-to-all | bytes 2359296 | tf_op jit(solution)/shard_map/all_to_all | solution.py:30
  37.9 0.0 copy-start.5
  37.9 0.9 sum_kernel.1
  38.8 12.7 %all-to-all-start.1 = ((bf16[48,12,128]{2,1,0:T(8,128)(2,1)}), bf16[48,12,128]{2,1,0:T(8,128)(2,1)S(1)}, u32[]{:S(2)}, u32[]{:S(2)}) async-start(bf16[48,12,128]{2,1,0:T(8,128)(2,1)} %sum_kernel.1), calls=%async_computation.1 | async-start | bytes 393216 | tf_op jit(solution)/shard_map/all_to_all | solution.py:30
  51.6 0.0 copy-done.5
  51.6 4.1 %collective-permute-start.1 = (f32[3,6,128]{2,1,0:T(8,128)S(1)}, f32[3,6,128]{2,1,0:T(8,128)S(1)}, u32[]{:S(2)}, u32[]{:S(2)}) collective-permute-start(f32[3,6,128]{2,1,0:T(8,128)S(1)} %copy-done.5), channel_id=1, source_target_pairs={{0,1},{1,0},{2,3},{3,2},{4,5},{5,4},{6,7},{7,6},{8,9},{9,8},{10,11... | collective-permute-start | bytes 27656 | tf_op jit(solution)/shard_map/ppermute | solution.py:241
  55.7 0.8 collective-permute-done.1
  56.5 9.2 %all-to-all-done.1.blocks = bf16[48,12,128]{2,1,0:T(8,128)(2,1)S(1)} async-done(((bf16[48,12,128]{2,1,0:T(8,128)(2,1)}), bf16[48,12,128]{2,1,0:T(8,128)(2,1)S(1)}, u32[]{:S(2)}, u32[]{:S(2)}) %all-to-all-start.1) | async-done | bytes 147488 | tf_op jit(solution)/shard_map/all_to_all | solution.py:30
  65.7 0.8 finish_kernel.1
  66.4 6.6 %all-to-all-start.2 = ((bf16[48,12,128]{2,1,0:T(8,128)(2,1)}), bf16[48,12,128]{2,1,0:T(8,128)(2,1)S(1)}, u32[]{:S(2)}, u32[]{:S(2)}) async-start(bf16[48,12,128]{2,1,0:T(8,128)(2,1)} %get-tuple-element.35), calls=%async_computation.2 | async-start | bytes 393216 | tf_op jit(solution)/shard_map/all_to_all | solution.py:30
  73.1 4.7 %collective-permute-start.2 = (f32[6,128]{1,0:T(8,128)S(1)}, f32[6,128]{1,0:T(8,128)S(1)}, u32[]{:S(2)}, u32[]{:S(2)}) collective-permute-start(f32[6,128]{1,0:T(8,128)S(1)} %slice_select_fusion), channel_id=1, source_target_pairs={{0,1},{1,0},{2,3},{3,2},{4,5},{5,4},{6,7},{7,6},{8,9},{9,8},{10,11... | collective-permute-start | bytes 9224 | tf_op jit(solution)/shard_map/ppermute | solution.py:248
  77.8 9.4 %all-to-all-done.2.blocks = bf16[48,12,128]{2,1,0:T(8,128)(2,1)S(1)} async-done(((bf16[48,12,128]{2,1,0:T(8,128)(2,1)}), bf16[48,12,128]{2,1,0:T(8,128)(2,1)S(1)}, u32[]{:S(2)}, u32[]{:S(2)}) %all-to-all-start.2) | async-done | bytes 147488 | tf_op jit(solution)/shard_map/all_to_all | solution.py:30
  87.2 0.1 spread_kernel.1
  87.3 0.0 collective-permute-done.2
  87.3 16.7 %all_to_all.21 = bf16[8,576,128]{2,1,0:T(8,128)(2,1)S(1)} all-to-all(bf16[8,576,128]{2,1,0:T(8,128)(2,1)S(1)} %spread_kernel.1), channel_id=1, replica_groups=mesh['yh'=2,'x'=4,'yl'=2,'yp'=2,'z'=12,'core'=2] {'x','yp'}, dimensions={0} | all-to-all | bytes 2359296 | tf_op jit(solution)/shard_map/all_to_all | solution.py:30
  104.0 6.9 %collective-permute-start.3 = (bf16[8,576,128]{2,1,0:T(8,128)(2,1)S(1)}, bf16[8,576,128]{2,1,0:T(8,128)(2,1)S(1)}, u32[]{:S(2)}, u32[]{:S(2)}) collective-permute-start(bf16[8,576,128]{2,1,0:T(8,128)(2,1)S(1)} %all_to_all.21), channel_id=1, source_target_pairs={{0,1},{1,0},{2,3},{3,2},{4,5},{5,4},{6,7},{7,6},{8,9},{9,8},{10,11... | collective-permute-start | bytes 3538952 | tf_op jit(solution)/shard_map/ppermute | solution.py:253
  111.0 0.0 copy-start.1
  111.0 0.0 copy-start.2
  111.0 0.0 copy-start.4
  111.0 1.1 write_kernel.2.refs_1_
  112.1 0.0 copy-done.1
  112.1 0.0 copy-done.2
  112.1 0.0 copy-done.4
  112.1 0.6 copy.17
  112.8 0.6 copy.18
  113.3 0.6 copy.19
  113.9 0.0 collective-permute-done.3
  113.9 1.1 write_kernel.3
  (7 shorter events, 0.1 us)
Async XLA Ops:
  3.5 14.9 %collective-permute-start = (bf16[8,576,128]{2,1,0:T(8,128)(2,1)S(1)}, bf16[8,576,128]{2,1,0:T(8,128)(2,1)S(1)}, u32[]{:S(2)}, u32[]{:S(2)}) collective-permute-start(bf16[8,576,128]{2,1,0:T(8,128)(2,1)S(1)} %get-tuple-element.27), channel_id=1, source_target_pairs={{0,1},{1,0},{2,3},{3,2},{4,5},{5,4},{6,7},{7,6},{8,9},{9,8},{10,11... | collective-permute-start | bytes 3538952 | tf_op jit(solution)/shard_map/ppermute | solution.py:231
  15.9 1.0 copy-start.3
  15.9 1.0 copy-start
  37.9 13.6 %copy-start.5 = (f32[3,6,128]{2,1,0:T(8,128)S(1)}, f32[3,6,128]{2,1,0:T(8,128)}, u32[]{:S(2)}) copy-start(f32[3,6,128]{2,1,0:T(8,128)} %get-tuple-element.33) | copy-start | bytes 27652
  38.8 26.8 %all-to-all-start.1 = ((bf16[48,12,128]{2,1,0:T(8,128)(2,1)}), bf16[48,12,128]{2,1,0:T(8,128)(2,1)S(1)}, u32[]{:S(2)}, u32[]{:S(2)}) async-start(bf16[48,12,128]{2,1,0:T(8,128)(2,1)} %sum_kernel.1), calls=%async_computation.1 | async-start | bytes 393216 | tf_op jit(solution)/shard_map/all_to_all | solution.py:30
  51.6 4.9 %collective-permute-start.1 = (f32[3,6,128]{2,1,0:T(8,128)S(1)}, f32[3,6,128]{2,1,0:T(8,128)S(1)}, u32[]{:S(2)}, u32[]{:S(2)}) collective-permute-start(f32[3,6,128]{2,1,0:T(8,128)S(1)} %copy-done.5), channel_id=1, source_target_pairs={{0,1},{1,0},{2,3},{3,2},{4,5},{5,4},{6,7},{7,6},{8,9},{9,8},{10,11... | collective-permute-start | bytes 27656 | tf_op jit(solution)/shard_map/ppermute | solution.py:241
  66.4 20.7 %all-to-all-start.2 = ((bf16[48,12,128]{2,1,0:T(8,128)(2,1)}), bf16[48,12,128]{2,1,0:T(8,128)(2,1)S(1)}, u32[]{:S(2)}, u32[]{:S(2)}) async-start(bf16[48,12,128]{2,1,0:T(8,128)(2,1)} %get-tuple-element.35), calls=%async_computation.2 | async-start | bytes 393216 | tf_op jit(solution)/shard_map/all_to_all | solution.py:30
  73.1 14.2 %collective-permute-start.2 = (f32[6,128]{1,0:T(8,128)S(1)}, f32[6,128]{1,0:T(8,128)S(1)}, u32[]{:S(2)}, u32[]{:S(2)}) collective-permute-start(f32[6,128]{1,0:T(8,128)S(1)} %slice_select_fusion), channel_id=1, source_target_pairs={{0,1},{1,0},{2,3},{3,2},{4,5},{5,4},{6,7},{7,6},{8,9},{9,8},{10,11... | collective-permute-start | bytes 9224 | tf_op jit(solution)/shard_map/ppermute | solution.py:248
  104.0 9.9 %collective-permute-start.3 = (bf16[8,576,128]{2,1,0:T(8,128)(2,1)S(1)}, bf16[8,576,128]{2,1,0:T(8,128)(2,1)S(1)}, u32[]{:S(2)}, u32[]{:S(2)}) collective-permute-start(bf16[8,576,128]{2,1,0:T(8,128)(2,1)S(1)} %all_to_all.21), channel_id=1, source_target_pairs={{0,1},{1,0},{2,3},{3,2},{4,5},{5,4},{6,7},{7,6},{8,9},{9,8},{10,11... | collective-permute-start | bytes 3538952 | tf_op jit(solution)/shard_map/ppermute | solution.py:253
  111.0 1.1 copy-start.1
  111.0 1.1 copy-start.2
  111.0 1.1 copy-start.4

commit v9 on v8

--- a/solution.py
+++ b/solution.py
@@ -10,7 +10,7 @@
 
 ALL = ("yh", "x", "yl", "yp", "z", "core")
 SIZES = (2, 4, 2, 2, 12, 2)
-NEAR = ("x", "yp")
+NEAR = ("yp", "x")
 FAR = ("yl", "z", "yh")
 SWAP = [(0, 1), (1, 0)]
 N_NEAR, N_FAR = 8, 48
@@ -32,7 +32,7 @@
 
 def place(block):
     yh, x, yl, yp = block // 16, block // 4 % 4, block // 2 % 2, block % 2
-    return x * 2 + yp, (yh * 2 + yl) * BLOCK
+    return yp * 4 + x, (yh * 2 + yl) * BLOCK
 
 
 def far_rows(index):
@@ -167,7 +167,7 @@
         for yp in range(2):
             copies.append(
                 pltpu.make_async_copy(
-                    blocks.at[x, yp], out.at[bucket, :, x, :, yp], done.at[x * 2 + yp]
+                    blocks.at[yp, x], out.at[bucket, :, x, :, yp], done.at[yp * 4 + x]
                 )
             )
             copies[-1].start()
@@ -178,7 +178,7 @@
 def write_bucket(blocks, other, out=None):
     shape = (2, 2, 4, 2, 2, BLOCK, COLS)
     whole = pl.BlockSpec(memory_space=pl.ANY)
-    blocks = blocks.reshape(4, 2, 2, 2, BLOCK, COLS)
+    blocks = blocks.reshape(2, 4, 2, 2, BLOCK, COLS)
     return pl.pallas_call(
         functools.partial(write_kernel, other),
         out_shape=jax.ShapeDtypeStruct(shape, jnp.bfloat16),

time: 115 us -> 115 us (level)
  no operation moved by 1% of the time
where the time goes in v9:
time: 115 us
  starting transfers between devices  48 us (42%)
  blocking collectives  35.3 us (31%)
  waiting for transfers between devices  19.6 us (17%)
  Pallas kernels  8.03 us (7%)
  local copies, waits for them, and re-layouts  2.53 us (2%)
    all_to_all x2, blocking collectives, exchange(): return lax.all_to_all(blocks, axes, 0, 0, tiled=True)  35.3 us
    all_to_all x2, starting transfers between devices, exchange(): return lax.all_to_all(blocks, axes, 0, 0, tiled=True)  19.8 us
    all_to_all x2, waiting for transfers between devices, exchange(): return lax.all_to_all(blocks, axes, 0, 0, tiled=True)  18.6 us
    ppermute x1, starting transfers between devices, on_device(): away = lax.ppermute(away, 'core', SWAP)  12.4 us
    ppermute x1, starting transfers between devices, on_device(): theirs = lax.ppermute(mine, 'core', SWAP)  7.15 us
    ppermute x1, starting transfers between devices, on_device(): lax.ppermute(jnp.where(first, gradient[6:], gradient[:6]), 'core', SWAP)  4.63 us
    ppermute x1, starting transfers between devices, on_device(): other_state = lax.ppermute(other_state, 'core', SWAP)  4.06 us
    pallas_call x1, Pallas kernels, first_gradient(): pl.pallas_call(first_kernel, out_shape=[NEAR_BLOCKS, pltpu.VMEM(tokens.sh...  2.85 us
  transfers between devices with their start and end apart: 6, of which 4 were waited for; matrix products, arithmetic and copies ran while one was open for 3% of the time, Pallas kernels for 2%

profile of v9, /device:TPU:1, one launch (start us, length us, event | category | flops | bytes accessed | tf_op | source)
XLA Modules:
  0.0 114.9 jit_solution(5506865314902943382)
XLA Ops:
  0.6 2.8 %first_kernel.1 = (bf16[8,576,128]{2,1,0:T(8,128)(2,1)S(1)}, bf16[384,4608]{1,0:T(8,128)(2,1)S(1)}, bf16[2,384,128]{2,1,0:T(8,128)(2,1)S(1)}) custom-call(bf16[384,4608]{1,0:T(8,128)(2,1)} %tokens.1, bf16[2,384,128]{2,1,0:T(8,128)(2,1)} %cotangents.1), custom_call_target="tpu_custom_call" | custom-call | tf_op jit(solution)/shard_map/first_kernel/pallas_call | solution.py:77
  3.5 12.4 %collective-permute-start = (bf16[8,576,128]{2,1,0:T(8,128)(2,1)S(1)}, bf16[8,576,128]{2,1,0:T(8,128)(2,1)S(1)}, u32[]{:S(2)}, u32[]{:S(2)}) collective-permute-start(bf16[8,576,128]{2,1,0:T(8,128)(2,1)S(1)} %get-tuple-element.27), channel_id=1, source_target_pairs={{0,1},{1,0},{2,3},{3,2},{4,5},{5,4},{6,7},{7,6},{8,9},{9,8},{10,11... | collective-permute-start | bytes 3538952 | tf_op jit(solution)/shard_map/ppermute | solution.py:231
  15.9 0.0 copy-start.3
  15.9 0.0 copy-start
  16.0 1.0 second_kernel.1.left
  16.9 0.0 copy-done.3
  16.9 0.0 copy-done
  17.0 0.7 copy_bitcast_fusion
  17.7 0.6 select_bitcast_fusion
  18.3 0.1 collective-permute-done.right
  18.4 0.3 add_kernel.1
  18.6 18.8 %all_to_all.20.blocks = bf16[8,576,128]{2,1,0:T(8,128)(2,1)S(1)} all-to-all(bf16[8,576,128]{2,1,0:T(8,128)(2,1)S(1)} %add_kernel.1), channel_id=1, replica_groups=mesh['yh'=2,'x'=4,'yl'=2,'yp'=2,'z'=12,'core'=2] {'yp','x'}, dimensions={0} | all-to-all | bytes 2359296 | tf_op jit(solution)/shard_map/all_to_all | solution.py:30
  37.4 0.0 copy-start.5
  37.4 0.9 sum_kernel.1
  38.3 13.1 %all-to-all-start.1 = ((bf16[48,12,128]{2,1,0:T(8,128)(2,1)}), bf16[48,12,128]{2,1,0:T(8,128)(2,1)S(1)}, u32[]{:S(2)}, u32[]{:S(2)}) async-start(bf16[48,12,128]{2,1,0:T(8,128)(2,1)} %sum_kernel.1), calls=%async_computation.1 | async-start | bytes 393216 | tf_op jit(solution)/shard_map/all_to_all | solution.py:30
  51.5 0.0 copy-done.5
  51.5 4.1 %collective-permute-start.1 = (f32[3,6,128]{2,1,0:T(8,128)S(1)}, f32[3,6,128]{2,1,0:T(8,128)S(1)}, u32[]{:S(2)}, u32[]{:S(2)}) collective-permute-start(f32[3,6,128]{2,1,0:T(8,128)S(1)} %copy-done.5), channel_id=1, source_target_pairs={{0,1},{1,0},{2,3},{3,2},{4,5},{5,4},{6,7},{7,6},{8,9},{9,8},{10,11... | collective-permute-start | bytes 27656 | tf_op jit(solution)/shard_map/ppermute | solution.py:241
  55.6 0.8 collective-permute-done.1
  56.4 9.2 %all-to-all-done.1.blocks = bf16[48,12,128]{2,1,0:T(8,128)(2,1)S(1)} async-done(((bf16[48,12,128]{2,1,0:T(8,128)(2,1)}), bf16[48,12,128]{2,1,0:T(8,128)(2,1)S(1)}, u32[]{:S(2)}, u32[]{:S(2)}) %all-to-all-start.1) | async-done | bytes 147488 | tf_op jit(solution)/shard_map/all_to_all | solution.py:30
  65.6 0.8 finish_kernel.1
  66.4 6.6 %all-to-all-start.2 = ((bf16[48,12,128]{2,1,0:T(8,128)(2,1)}), bf16[48,12,128]{2,1,0:T(8,128)(2,1)S(1)}, u32[]{:S(2)}, u32[]{:S(2)}) async-start(bf16[48,12,128]{2,1,0:T(8,128)(2,1)} %get-tuple-element.35), calls=%async_computation.2 | async-start | bytes 393216 | tf_op jit(solution)/shard_map/all_to_all | solution.py:30
  73.0 4.6 %collective-permute-start.2 = (f32[6,128]{1,0:T(8,128)S(1)}, f32[6,128]{1,0:T(8,128)S(1)}, u32[]{:S(2)}, u32[]{:S(2)}) collective-permute-start(f32[6,128]{1,0:T(8,128)S(1)} %slice_select_fusion), channel_id=1, source_target_pairs={{0,1},{1,0},{2,3},{3,2},{4,5},{5,4},{6,7},{7,6},{8,9},{9,8},{10,11... | collective-permute-start | bytes 9224 | tf_op jit(solution)/shard_map/ppermute | solution.py:248
  77.7 9.4 %all-to-all-done.2.blocks = bf16[48,12,128]{2,1,0:T(8,128)(2,1)S(1)} async-done(((bf16[48,12,128]{2,1,0:T(8,128)(2,1)}), bf16[48,12,128]{2,1,0:T(8,128)(2,1)S(1)}, u32[]{:S(2)}, u32[]{:S(2)}) %all-to-all-start.2) | async-done | bytes 147488 | tf_op jit(solution)/shard_map/all_to_all | solution.py:30
  87.1 0.1 spread_kernel.1
  87.2 0.0 collective-permute-done.2
  87.2 16.5 %all_to_all.21 = bf16[8,576,128]{2,1,0:T(8,128)(2,1)S(1)} all-to-all(bf16[8,576,128]{2,1,0:T(8,128)(2,1)S(1)} %spread_kernel.1), channel_id=1, replica_groups=mesh['yh'=2,'x'=4,'yl'=2,'yp'=2,'z'=12,'core'=2] {'yp','x'}, dimensions={0} | all-to-all | bytes 2359296 | tf_op jit(solution)/shard_map/all_to_all | solution.py:30
  103.7 7.1 %collective-permute-start.3 = (bf16[8,576,128]{2,1,0:T(8,128)(2,1)S(1)}, bf16[8,576,128]{2,1,0:T(8,128)(2,1)S(1)}, u32[]{:S(2)}, u32[]{:S(2)}) collective-permute-start(bf16[8,576,128]{2,1,0:T(8,128)(2,1)S(1)} %all_to_all.21), channel_id=1, source_target_pairs={{0,1},{1,0},{2,3},{3,2},{4,5},{5,4},{6,7},{7,6},{8,9},{9,8},{10,11... | collective-permute-start | bytes 3538952 | tf_op jit(solution)/shard_map/ppermute | solution.py:253
  110.9 0.0 copy-start.1
  110.9 0.0 copy-start.2
  110.9 0.0 copy-start.4
  110.9 1.1 write_kernel.2.refs_1_
  112.0 0.0 copy-done.1
  112.0 0.0 copy-done.2
  112.0 0.0 copy-done.4
  112.1 0.6 copy.17
  112.7 0.6 copy.18
  113.3 0.6 copy.19
  113.9 0.0 collective-permute-done.3
  113.9 1.1 write_kernel.3
  (7 shorter events, 0.1 us)
Async XLA Ops:
  3.5 14.9 %collective-permute-start = (bf16[8,576,128]{2,1,0:T(8,128)(2,1)S(1)}, bf16[8,576,128]{2,1,0:T(8,128)(2,1)S(1)}, u32[]{:S(2)}, u32[]{:S(2)}) collective-permute-start(bf16[8,576,128]{2,1,0:T(8,128)(2,1)S(1)} %get-tuple-element.27), channel_id=1, source_target_pairs={{0,1},{1,0},{2,3},{3,2},{4,5},{5,4},{6,7},{7,6},{8,9},{9,8},{10,11... | collective-permute-start | bytes 3538952 | tf_op jit(solution)/shard_map/ppermute | solution.py:231
  15.9 1.0 copy-start.3
  15.9 1.0 copy-start
  37.4 14.1 %copy-start.5 = (f32[3,6,128]{2,1,0:T(8,128)S(1)}, f32[3,6,128]{2,1,0:T(8,128)}, u32[]{:S(2)}) copy-start(f32[3,6,128]{2,1,0:T(8,128)} %get-tuple-element.33) | copy-start | bytes 27652
  38.3 27.3 %all-to-all-start.1 = ((bf16[48,12,128]{2,1,0:T(8,128)(2,1)}), bf16[48,12,128]{2,1,0:T(8,128)(2,1)S(1)}, u32[]{:S(2)}, u32[]{:S(2)}) async-start(bf16[48,12,128]{2,1,0:T(8,128)(2,1)} %sum_kernel.1), calls=%async_computation.1 | async-start | bytes 393216 | tf_op jit(solution)/shard_map/all_to_all | solution.py:30
  51.5 4.9 %collective-permute-start.1 = (f32[3,6,128]{2,1,0:T(8,128)S(1)}, f32[3,6,128]{2,1,0:T(8,128)S(1)}, u32[]{:S(2)}, u32[]{:S(2)}) collective-permute-start(f32[3,6,128]{2,1,0:T(8,128)S(1)} %copy-done.5), channel_id=1, source_target_pairs={{0,1},{1,0},{2,3},{3,2},{4,5},{5,4},{6,7},{7,6},{8,9},{9,8},{10,11... | collective-permute-start | bytes 27656 | tf_op jit(solution)/shard_map/ppermute | solution.py:241
  66.4 20.7 %all-to-all-start.2 = ((bf16[48,12,128]{2,1,0:T(8,128)(2,1)}), bf16[48,12,128]{2,1,0:T(8,128)(2,1)S(1)}, u32[]{:S(2)}, u32[]{:S(2)}) async-start(bf16[48,12,128]{2,1,0:T(8,128)(2,1)} %get-tuple-element.35), calls=%async_computation.2 | async-start | bytes 393216 | tf_op jit(solution)/shard_map/all_to_all | solution.py:30
  73.0 14.2 %collective-permute-start.2 = (f32[6,128]{1,0:T(8,128)S(1)}, f32[6,128]{1,0:T(8,128)S(1)}, u32[]{:S(2)}, u32[]{:S(2)}) collective-permute-start(f32[6,128]{1,0:T(8,128)S(1)} %slice_select_fusion), channel_id=1, source_target_pairs={{0,1},{1,0},{2,3},{3,2},{4,5},{5,4},{6,7},{7,6},{8,9},{9,8},{10,11... | collective-permute-start | bytes 9224 | tf_op jit(solution)/shard_map/ppermute | solution.py:248
  103.7 10.2 %collective-permute-start.3 = (bf16[8,576,128]{2,1,0:T(8,128)(2,1)S(1)}, bf16[8,576,128]{2,1,0:T(8,128)(2,1)S(1)}, u32[]{:S(2)}, u32[]{:S(2)}) collective-permute-start(bf16[8,576,128]{2,1,0:T(8,128)(2,1)S(1)} %all_to_all.21), channel_id=1, source_target_pairs={{0,1},{1,0},{2,3},{3,2},{4,5},{5,4},{6,7},{7,6},{8,9},{9,8},{10,11... | collective-permute-start | bytes 3538952 | tf_op jit(solution)/shard_map/ppermute | solution.py:253
  110.9 1.1 copy-start.1
  110.9 1.1 copy-start.2
  110.9 1.1 copy-start.4
